TPU v7x, 32 devices: a whole 2x2x4 slice. The times are simulated.
32 devices in a mesh: space: 4 (over y, x), tm: 8 (over z, core).
Axes of the slice: x: 2, y: 2, z: 4, core: 2. Of those that a mesh axis runs over, the one named last changes fastest.
Arguments:
- forcing: float32 [16, 96, 20, 128], P('tm', 'space'), may hold values from -6 to 6
- observed: float32 [16, 96, 20, 128], P('tm', 'space'), may hold values from -6 to 6
- jacobian: bfloat16 [16, 96, 7, 128, 128], P('tm', 'space'), may hold values from -0.078125 to 0.078125
- block_index: int32 [96, 7], P('space'), may hold values from 0 to 27, as said below
- send_list: int32 [16, 1], P('space'), may hold values from 0 to 23
- damping: float32 [96, 128], P('space'), may hold values from 0.5 to 0.9
- error_weight: float32 [96, 128], P('space'), may hold values from 0.5 to 2
- forcing_weight: float32 [128], replicated, may hold values from 0.5 to 2
Outputs:
- trajectory: float32 [16, 96, 20, 128], P('tm', 'space')
- gradient: float32 [16, 96, 20, 128], P('tm', 'space')
Inputs may be any that keep to these rules, and one draw needn't show every extreme that they name: `block_index`: block 0 of every column reads the column itself; each received column is read by exactly one block of its partition.
All inputs are finite; a program needn't handle non-finite values.
Results may differ from a plain program's by a relative error of at most 0.0045.
Values may be sent and summed in bfloat16 or wider, within the bound.
A program may use at most 64 MiB of HBM per device.

v0:
```python
import jax
import jax.numpy as jnp
from jax import lax
from jax.sharding import PartitionSpec as P

OFFSETS = (1, -1, 2, -2)


def from_behind(array, axis, by):
    devices = lax.axis_size(axis)
    return lax.ppermute(array, axis, [(i, (i + by) % devices) for i in range(devices)])


def shifted(block, axis, distance):
    devices = range(lax.axis_size(axis))
    route = [(i - distance, i) for i in devices if i - distance in devices]
    return lax.ppermute(block, axis, route)


def send_border(piece, offset):
    return from_behind(piece, "space", offset)


def return_border(piece, offset):
    return from_behind(piece, "space", -offset)


def forward_step(current, push, blocks, damping, block_index, send_list):
    rounded = current.astype(jnp.bfloat16)
    pieces = [rounded]
    for hop_id in range(send_list.shape[0]):
        pieces.append(send_border(rounded[send_list[hop_id]], OFFSETS[hop_id]))
    extended = jnp.concatenate(pieces, axis=0)
    picked = extended[block_index]
    mixed = jnp.einsum("ckmj,ckij->cmi", picked, blocks, preferred_element_type=jnp.float32)
    return damping[:, None, :] * current + mixed + push


def adjoint_step(adjoint, blocks, damping, block_index, send_list):
    rounded = adjoint.astype(jnp.bfloat16)
    spread = jnp.einsum("cmi,ckij->ckmj", rounded, blocks, preferred_element_type=jnp.float32)
    column_count = adjoint.shape[0]
    border_width = send_list.shape[1]
    listed = send_list.shape[0] * border_width
    totals = jax.ops.segment_sum(
        spread.reshape((-1,) + adjoint.shape[1:]),
        block_index.reshape(-1),
        num_segments=column_count + listed,
    )
    result = damping[:, None, :] * adjoint + totals[:column_count]
    for hop_id in range(send_list.shape[0]):
        first = column_count + hop_id * border_width
        back = return_border(totals[first : first + border_width], OFFSETS[hop_id])
        result = result + jax.ops.segment_sum(back, send_list[hop_id], num_segments=column_count)
    return result


def run_forward(carried, pushes, jacobian, damping, block_index, send_list):
    current = carried
    states = []
    for position in range(pushes.shape[0]):
        current = forward_step(
            current, pushes[position], jacobian[position], damping, block_index, send_list
        )
        states.append(current)
    return (jnp.stack(states), current)


def run_adjoint(carried, misses, jacobian, damping, block_index, send_list):
    steps_here = misses.shape[0]
    adjoint = misses[steps_here - 1] + carried
    values = [adjoint]
    adjoint = misses[0] + adjoint_step(adjoint, jacobian[1], damping, block_index, send_list)
    values.append(adjoint)
    ordered = values[::-1]
    handed = adjoint_step(adjoint, jacobian[0], damping, block_index, send_list)
    return (jnp.stack(ordered), handed)


def on_device(
    forcing, observed, jacobian, block_index, send_list, damping, error_weight, forcing_weight
):
    count = lax.axis_size("tm")
    shared = (jacobian, damping, block_index, send_list)

    def forward_turn(turn_no, carried):
        unused, final_state = run_forward(carried, forcing, *shared)
        return shifted(final_state, "tm", 1)

    carried = lax.fori_loop(0, count - 1, forward_turn, jnp.zeros(forcing.shape[1:], jnp.float32))
    trajectory, unused = run_forward(carried, forcing, *shared)
    misfit = error_weight[:, None, :] * (trajectory - observed)

    def adjoint_turn(turn_no, carried):
        unused, handed = run_adjoint(carried, misfit, *shared)
        return shifted(handed, "tm", -1)

    carried = lax.fori_loop(0, count - 1, adjoint_turn, jnp.zeros(forcing.shape[1:], jnp.float32))
    adjoints, unused = run_adjoint(carried, misfit, *shared)
    gradient = forcing_weight * forcing + adjoints
    return (trajectory, gradient)


def solution(mesh):
    in_specs = (
        P("tm", "space", None, None),
        P("tm", "space", None, None),
        P("tm", "space", None, None, None),
        P("space", None),
        P("space", None),
        P("space", None),
        P("space", None),
        P(),
    )
    out_specs = (P("tm", "space", None, None), P("tm", "space", None, None))
    return jax.shard_map(
        on_device, mesh=mesh, in_specs=in_specs, out_specs=out_specs, check_vma=False
    )
```

profile of v0, /device:TPU:0, one launch (start us, length us, event | category | flops | bytes accessed | tf_op | source)
XLA Modules:
  0.0 654.3 jit_solution(11873539659319036046)
XLA Ops:
  11.5 228.4 %while.54 = (s32[]{:T(128)}, f32[24,20,128]{2,1,0:T(8,128)S(1)}, f32[24,128]{1,0:T(8,128)}, s32[1]{0:T(128)}, s32[1]{0:T(128)}, /*index=5*/s32[1]{0:T(128)}, s32...) while((s32[]{:T(128)}, f32[24,20,128]{2,1,0:T(8,128)S(1)}, ...), condition=%wide.region_1.0_spmd, body=%wide.region_0.0_spmd.sunk | while | flops 220694016 | bytes 19940464 | solution.py:90
  92.3 4.3 fusion.106
  96.6 6.9 %collective-permute-start.8 = (f32[24,20,128]{2,1,0:T(8,128)S(1)}, f32[24,20,128]{2,1,0:T(8,128)S(1)}, u32[]{:S(2)}, u32[]{:S(2)}) collective-permute-start(f32[24,20,128]{2,1,0:T(8,128)S(1)} %fusion.106), channel_id=1, source_target_pairs={{0,1},{1,2},{2,3},{3,4},{4,5},{5,6},{6,7},{8,9},{9,10},{10,11},{11... | collective-permute-start | bytes 737288 | tf_op jit(solution)/shard_map/while/body/eval_jaxpr/ppermute | solution.py:17
  130.4 6.9 %collective-permute-start.8 = (f32[24,20,128]{2,1,0:T(8,128)S(1)}, f32[24,20,128]{2,1,0:T(8,128)S(1)}, u32[]{:S(2)}, u32[]{:S(2)}) collective-permute-start(f32[24,20,128]{2,1,0:T(8,128)S(1)} %fusion.106), channel_id=1, source_target_pairs={{0,1},{1,2},{2,3},{3,4},{4,5},{5,6},{6,7},{8,9},{9,10},{10,11},{11... | collective-permute-start | bytes 737288 | tf_op jit(solution)/shard_map/while/body/eval_jaxpr/ppermute | solution.py:17
  164.2 6.9 %collective-permute-start.8 = (f32[24,20,128]{2,1,0:T(8,128)S(1)}, f32[24,20,128]{2,1,0:T(8,128)S(1)}, u32[]{:S(2)}, u32[]{:S(2)}) collective-permute-start(f32[24,20,128]{2,1,0:T(8,128)S(1)} %fusion.106), channel_id=1, source_target_pairs={{0,1},{1,2},{2,3},{3,4},{4,5},{5,6},{6,7},{8,9},{9,10},{10,11},{11... | collective-permute-start | bytes 737288 | tf_op jit(solution)/shard_map/while/body/eval_jaxpr/ppermute | solution.py:17
  193.7 4.3 fusion.106
  198.0 6.9 %collective-permute-start.8 = (f32[24,20,128]{2,1,0:T(8,128)S(1)}, f32[24,20,128]{2,1,0:T(8,128)S(1)}, u32[]{:S(2)}, u32[]{:S(2)}) collective-permute-start(f32[24,20,128]{2,1,0:T(8,128)S(1)} %fusion.106), channel_id=1, source_target_pairs={{0,1},{1,2},{2,3},{3,4},{4,5},{5,6},{6,7},{8,9},{9,10},{10,11},{11... | collective-permute-start | bytes 737288 | tf_op jit(solution)/shard_map/while/body/eval_jaxpr/ppermute | solution.py:17
  231.8 6.9 %collective-permute-start.8 = (f32[24,20,128]{2,1,0:T(8,128)S(1)}, f32[24,20,128]{2,1,0:T(8,128)S(1)}, u32[]{:S(2)}, u32[]{:S(2)}) collective-permute-start(f32[24,20,128]{2,1,0:T(8,128)S(1)} %fusion.106), channel_id=1, source_target_pairs={{0,1},{1,2},{2,3},{3,4},{4,5},{5,6},{6,7},{8,9},{9,10},{10,11},{11... | collective-permute-start | bytes 737288 | tf_op jit(solution)/shard_map/while/body/eval_jaxpr/ppermute | solution.py:17
  265.0 4.3 fusion.55
  270.4 359.3 %while.55 = (s32[]{:T(128)}, f32[24,20,128]{2,1,0:T(8,128)S(1)}, f32[24,128]{1,0:T(8,128)S(1)}, f32[2,24,20,128]{3,2,1,0:T(8,128)S(1)}, s32[24,7]{1,0:T(8,128)},...) while((s32[]{:T(128)}, f32[24,20,128]{2,1,0:T(8,128)S(1)}, ...), condition=%wide.wide.region_9.10_spmd, body=%wide.wide.region_6.9_spmd.sunk | while | flops 221716480 | bytes 31270804 | solution.py:98
  274.0 7.7 %scatter_fusion = f32[28,20,128]{2,1,0:T(8,128)S(1)} fusion(f32[28,20,128]{2,1,0:T(8,128)S(1)} %broadcast.642.clone, s32[168]{0:T(256)S(1)} %get-tuple-element.1038, f32[168,20,128]{2,1,0:T(8,128)S(1)} %bitcast.255), kind=kCustom, calls=%fused_computation.4.clone.clone.1 | custom fusion | flops 430080 | bytes 5161632 | tf_op jit(solution)/shard_map/while/body/eval_jaxpr/scatter-add | solution.py:45
  296.1 7.7 %scatter_fusion.1 = f32[28,20,128]{2,1,0:T(8,128)S(1)} fusion(f32[28,20,128]{2,1,0:T(8,128)S(1)} %broadcast.642, s32[168]{0:T(256)S(1)} %get-tuple-element.1038, f32[168,20,128]{2,1,0:T(8,128)S(1)} %bitcast.254), kind=kCustom, calls=%fused_computation.5.clone.clone.1 | custom fusion | flops 430080 | bytes 5161632 | tf_op jit(solution)/shard_map/while/body/eval_jaxpr/scatter-add | solution.py:45
  315.0 4.6 collective-permute-done.17
  323.2 7.7 %scatter_fusion = f32[28,20,128]{2,1,0:T(8,128)S(1)} fusion(f32[28,20,128]{2,1,0:T(8,128)S(1)} %broadcast.642.clone, s32[168]{0:T(256)S(1)} %get-tuple-element.1038, f32[168,20,128]{2,1,0:T(8,128)S(1)} %bitcast.255), kind=kCustom, calls=%fused_computation.4.clone.clone.1 | custom fusion | flops 430080 | bytes 5161632 | tf_op jit(solution)/shard_map/while/body/eval_jaxpr/scatter-add | solution.py:45
  345.3 7.7 %scatter_fusion.1 = f32[28,20,128]{2,1,0:T(8,128)S(1)} fusion(f32[28,20,128]{2,1,0:T(8,128)S(1)} %broadcast.642, s32[168]{0:T(256)S(1)} %get-tuple-element.1038, f32[168,20,128]{2,1,0:T(8,128)S(1)} %bitcast.254), kind=kCustom, calls=%fused_computation.5.clone.clone.1 | custom fusion | flops 430080 | bytes 5161632 | tf_op jit(solution)/shard_map/while/body/eval_jaxpr/scatter-add | solution.py:45
  365.8 10.6 %collective-permute-done.17 = f32[24,20,128]{2,1,0:T(8,128)S(1)} collective-permute-done((f32[24,20,128]{2,1,0:T(8,128)S(1)}, f32[24,20,128]{2,1,0:T(8,128)S(1)}, u32[]{:S(2)}, u32[]{:S(2)}) %collective-permute-start.17) | collective-permute-done | bytes 245792 | tf_op jit(solution)/shard_map/while/body/eval_jaxpr/ppermute | solution.py:17
  380.0 7.7 %scatter_fusion = f32[28,20,128]{2,1,0:T(8,128)S(1)} fusion(f32[28,20,128]{2,1,0:T(8,128)S(1)} %broadcast.642.clone, s32[168]{0:T(256)S(1)} %get-tuple-element.1038, f32[168,20,128]{2,1,0:T(8,128)S(1)} %bitcast.255), kind=kCustom, calls=%fused_computation.4.clone.clone.1 | custom fusion | flops 430080 | bytes 5161632 | tf_op jit(solution)/shard_map/while/body/eval_jaxpr/scatter-add | solution.py:45
  402.0 7.7 %scatter_fusion.1 = f32[28,20,128]{2,1,0:T(8,128)S(1)} fusion(f32[28,20,128]{2,1,0:T(8,128)S(1)} %broadcast.642, s32[168]{0:T(256)S(1)} %get-tuple-element.1038, f32[168,20,128]{2,1,0:T(8,128)S(1)} %bitcast.254), kind=kCustom, calls=%fused_computation.5.clone.clone.1 | custom fusion | flops 430080 | bytes 5161632 | tf_op jit(solution)/shard_map/while/body/eval_jaxpr/scatter-add | solution.py:45
  422.5 4.6 collective-permute-done.17
  430.7 7.7 %scatter_fusion = f32[28,20,128]{2,1,0:T(8,128)S(1)} fusion(f32[28,20,128]{2,1,0:T(8,128)S(1)} %broadcast.642.clone, s32[168]{0:T(256)S(1)} %get-tuple-element.1038, f32[168,20,128]{2,1,0:T(8,128)S(1)} %bitcast.255), kind=kCustom, calls=%fused_computation.4.clone.clone.1 | custom fusion | flops 430080 | bytes 5161632 | tf_op jit(solution)/shard_map/while/body/eval_jaxpr/scatter-add | solution.py:45
  452.8 7.7 %scatter_fusion.1 = f32[28,20,128]{2,1,0:T(8,128)S(1)} fusion(f32[28,20,128]{2,1,0:T(8,128)S(1)} %broadcast.642, s32[168]{0:T(256)S(1)} %get-tuple-element.1038, f32[168,20,128]{2,1,0:T(8,128)S(1)} %bitcast.254), kind=kCustom, calls=%fused_computation.5.clone.clone.1 | custom fusion | flops 430080 | bytes 5161632 | tf_op jit(solution)/shard_map/while/body/eval_jaxpr/scatter-add | solution.py:45
  473.1 4.6 collective-permute-done.17
  481.4 7.7 %scatter_fusion = f32[28,20,128]{2,1,0:T(8,128)S(1)} fusion(f32[28,20,128]{2,1,0:T(8,128)S(1)} %broadcast.642.clone, s32[168]{0:T(256)S(1)} %get-tuple-element.1038, f32[168,20,128]{2,1,0:T(8,128)S(1)} %bitcast.255), kind=kCustom, calls=%fused_computation.4.clone.clone.1 | custom fusion | flops 430080 | bytes 5161632 | tf_op jit(solution)/shard_map/while/body/eval_jaxpr/scatter-add | solution.py:45
  503.4 7.7 %scatter_fusion.1 = f32[28,20,128]{2,1,0:T(8,128)S(1)} fusion(f32[28,20,128]{2,1,0:T(8,128)S(1)} %broadcast.642, s32[168]{0:T(256)S(1)} %get-tuple-element.1038, f32[168,20,128]{2,1,0:T(8,128)S(1)} %bitcast.254), kind=kCustom, calls=%fused_computation.5.clone.clone.1 | custom fusion | flops 430080 | bytes 5161632 | tf_op jit(solution)/shard_map/while/body/eval_jaxpr/scatter-add | solution.py:45
  523.8 4.6 collective-permute-done.17
  532.0 7.7 %scatter_fusion = f32[28,20,128]{2,1,0:T(8,128)S(1)} fusion(f32[28,20,128]{2,1,0:T(8,128)S(1)} %broadcast.642.clone, s32[168]{0:T(256)S(1)} %get-tuple-element.1038, f32[168,20,128]{2,1,0:T(8,128)S(1)} %bitcast.255), kind=kCustom, calls=%fused_computation.4.clone.clone.1 | custom fusion | flops 430080 | bytes 5161632 | tf_op jit(solution)/shard_map/while/body/eval_jaxpr/scatter-add | solution.py:45
  554.1 7.7 %scatter_fusion.1 = f32[28,20,128]{2,1,0:T(8,128)S(1)} fusion(f32[28,20,128]{2,1,0:T(8,128)S(1)} %broadcast.642, s32[168]{0:T(256)S(1)} %get-tuple-element.1038, f32[168,20,128]{2,1,0:T(8,128)S(1)} %bitcast.254), kind=kCustom, calls=%fused_computation.5.clone.clone.1 | custom fusion | flops 430080 | bytes 5161632 | tf_op jit(solution)/shard_map/while/body/eval_jaxpr/scatter-add | solution.py:45
  574.5 4.5 collective-permute-done.17
  582.7 7.7 %scatter_fusion = f32[28,20,128]{2,1,0:T(8,128)S(1)} fusion(f32[28,20,128]{2,1,0:T(8,128)S(1)} %broadcast.642.clone, s32[168]{0:T(256)S(1)} %get-tuple-element.1038, f32[168,20,128]{2,1,0:T(8,128)S(1)} %bitcast.255), kind=kCustom, calls=%fused_computation.4.clone.clone.1 | custom fusion | flops 430080 | bytes 5161632 | tf_op jit(solution)/shard_map/while/body/eval_jaxpr/scatter-add | solution.py:45
  604.7 7.7 %scatter_fusion.1 = f32[28,20,128]{2,1,0:T(8,128)S(1)} fusion(f32[28,20,128]{2,1,0:T(8,128)S(1)} %broadcast.642, s32[168]{0:T(256)S(1)} %get-tuple-element.1038, f32[168,20,128]{2,1,0:T(8,128)S(1)} %bitcast.254), kind=kCustom, calls=%fused_computation.5.clone.clone.1 | custom fusion | flops 430080 | bytes 5161632 | tf_op jit(solution)/shard_map/while/body/eval_jaxpr/scatter-add | solution.py:45
  625.1 4.5 collective-permute-done.17
  633.2 7.7 %scatter_fusion.2 = f32[28,20,128]{2,1,0:T(8,128)S(1)} fusion(f32[28,20,128]{2,1,0:T(8,128)S(1)} %broadcast.294, s32[168]{0:T(256)S(1)} %reshape.818, f32[168,20,128]{2,1,0:T(8,128)S(1)} %bitcast.258), kind=kCustom, calls=%fused_computation.6 | custom fusion | flops 430080 | bytes 5161632 | tf_op jit(solution)/shard_map/scatter-add | solution.py:45
  (590 shorter events, 443.4 us)
Async XLA Ops:
  11.6 6.2 collective-permute-start
  96.6 8.0 %collective-permute-start.8 = (f32[24,20,128]{2,1,0:T(8,128)S(1)}, f32[24,20,128]{2,1,0:T(8,128)S(1)}, u32[]{:S(2)}, u32[]{:S(2)}) collective-permute-start(f32[24,20,128]{2,1,0:T(8,128)S(1)} %fusion.106), channel_id=1, source_target_pairs={{0,1},{1,2},{2,3},{3,4},{4,5},{5,6},{6,7},{8,9},{9,10},{10,11},{11... | collective-permute-start | bytes 737288 | tf_op jit(solution)/shard_map/while/body/eval_jaxpr/ppermute | solution.py:17
  130.4 8.0 %collective-permute-start.8 = (f32[24,20,128]{2,1,0:T(8,128)S(1)}, f32[24,20,128]{2,1,0:T(8,128)S(1)}, u32[]{:S(2)}, u32[]{:S(2)}) collective-permute-start(f32[24,20,128]{2,1,0:T(8,128)S(1)} %fusion.106), channel_id=1, source_target_pairs={{0,1},{1,2},{2,3},{3,4},{4,5},{5,6},{6,7},{8,9},{9,10},{10,11},{11... | collective-permute-start | bytes 737288 | tf_op jit(solution)/shard_map/while/body/eval_jaxpr/ppermute | solution.py:17
  164.2 8.0 %collective-permute-start.8 = (f32[24,20,128]{2,1,0:T(8,128)S(1)}, f32[24,20,128]{2,1,0:T(8,128)S(1)}, u32[]{:S(2)}, u32[]{:S(2)}) collective-permute-start(f32[24,20,128]{2,1,0:T(8,128)S(1)} %fusion.106), channel_id=1, source_target_pairs={{0,1},{1,2},{2,3},{3,4},{4,5},{5,6},{6,7},{8,9},{9,10},{10,11},{11... | collective-permute-start | bytes 737288 | tf_op jit(solution)/shard_map/while/body/eval_jaxpr/ppermute | solution.py:17
  198.0 8.0 %collective-permute-start.8 = (f32[24,20,128]{2,1,0:T(8,128)S(1)}, f32[24,20,128]{2,1,0:T(8,128)S(1)}, u32[]{:S(2)}, u32[]{:S(2)}) collective-permute-start(f32[24,20,128]{2,1,0:T(8,128)S(1)} %fusion.106), channel_id=1, source_target_pairs={{0,1},{1,2},{2,3},{3,4},{4,5},{5,6},{6,7},{8,9},{9,10},{10,11},{11... | collective-permute-start | bytes 737288 | tf_op jit(solution)/shard_map/while/body/eval_jaxpr/ppermute | solution.py:17
  231.8 8.0 %collective-permute-start.8 = (f32[24,20,128]{2,1,0:T(8,128)S(1)}, f32[24,20,128]{2,1,0:T(8,128)S(1)}, u32[]{:S(2)}, u32[]{:S(2)}) collective-permute-start(f32[24,20,128]{2,1,0:T(8,128)S(1)} %fusion.106), channel_id=1, source_target_pairs={{0,1},{1,2},{2,3},{3,4},{4,5},{5,6},{6,7},{8,9},{9,10},{10,11},{11... | collective-permute-start | bytes 737288 | tf_op jit(solution)/shard_map/while/body/eval_jaxpr/ppermute | solution.py:17
  253.3 8.7 %collective-permute-start.22 = (bf16[1,20,128]{2,1,0:T(8,128)(2,1)S(1)}, bf16[1,20,128]{2,1,0:T(8,128)(2,1)S(1)}, u32[]{:S(2)}, u32[]{:S(2)}) collective-permute-start(bf16[1,20,128]{2,1,0:T(8,128)(2,1)S(1)} %get-tuple-element.714), channel_id=1, source_target_pairs={{0,8},{8,16},{16,24},{24,0},{1,9},{9,17},{17,25},{25,1},{2,10},{10... | collective-permute-start | bytes 15368 | tf_op jit(solution)/shard_map/ppermute | solution.py:11
  282.2 6.5 collective-permute-start.10
  283.8 6.2 collective-permute-start.11
  285.3 6.0 collective-permute-start.12
  333.0 6.2 collective-permute-start.11
  333.9 6.6 %collective-permute-start.12 = (f32[1,20,128]{2,1,0:T(8,128)S(1)}, f32[1,20,128]{2,1,0:T(8,128)S(1)}, u32[]{:S(2)}, u32[]{:S(2)}) collective-permute-start(f32[1,20,128]{2,1,0:T(8,128)S(1)} %get-tuple-element.961), channel_id=1, source_target_pairs={{0,16},{8,24},{16,0},{24,8},{1,17},{9,25},{17,1},{25,9},{2,18},{10... | collective-permute-start | bytes 30728 | tf_op jit(solution)/shard_map/while/body/eval_jaxpr/ppermute | solution.py:11
  356.9 6.3 collective-permute-start.16
  364.4 11.9 %collective-permute-start.17 = (f32[24,20,128]{2,1,0:T(8,128)S(1)}, f32[24,20,128]{2,1,0:T(8,128)S(1)}, u32[]{:S(2)}, u32[]{:S(2)}) collective-permute-start(f32[24,20,128]{2,1,0:T(8,128)S(1)} %add_dynamic-update-slice_fusion.35), channel_id=1, source_target_pairs={{1,0},{2,1},{3,2},{4,3},{5,4},{6,5},{7,6},{9,8},{10,9},{11,10},{12... | collective-permute-start | bytes 737288 | tf_op jit(solution)/shard_map/while/body/eval_jaxpr/ppermute | solution.py:17
  389.8 6.2 collective-permute-start.11
  390.9 6.4 collective-permute-start.12
  413.9 6.0 collective-permute-start.16
  440.5 6.2 collective-permute-start.11
  441.5 6.5 collective-permute-start.12
  464.5 6.0 collective-permute-start.16
  491.1 6.2 collective-permute-start.11
  492.2 6.5 collective-permute-start.12
  515.2 6.1 collective-permute-start.16
  541.8 6.2 collective-permute-start.11
  542.8 6.5 collective-permute-start.12
  565.8 6.1 collective-permute-start.16
  592.4 6.2 collective-permute-start.11
  593.5 6.4 collective-permute-start.12
  616.4 6.2 collective-permute-start.16
  640.9 6.2 collective-permute-start.26
  643.1 6.5 %collective-permute-start.28 = (f32[1,20,128]{2,1,0:T(8,128)S(1)}, f32[1,20,128]{2,1,0:T(8,128)S(1)}, u32[]{:S(2)}, u32[]{:S(2)}) collective-permute-start(f32[1,20,128]{2,1,0:T(8,128)S(1)} %get-tuple-element.708), channel_id=1, source_target_pairs={{0,16},{8,24},{16,0},{24,8},{1,17},{9,25},{17,1},{25,9},{2,18},{10... | collective-permute-start | bytes 30728 | tf_op jit(solution)/shard_map/ppermute | solution.py:11
  644.0 6.9 %collective-permute-start.29 = (f32[1,20,128]{2,1,0:T(8,128)S(1)}, f32[1,20,128]{2,1,0:T(8,128)S(1)}, u32[]{:S(2)}, u32[]{:S(2)}) collective-permute-start(f32[1,20,128]{2,1,0:T(8,128)S(1)} %get-tuple-element.707), channel_id=1, source_target_pairs={{0,16},{8,24},{16,0},{24,8},{1,17},{9,25},{17,1},{25,9},{2,18},{10... | collective-permute-start | bytes 30728 | tf_op jit(solution)/shard_map/ppermute | solution.py:11
  (128 other events, 1010.4 us)
where the time goes:
time: 661 us; the launch traced here: 654 us
  other arithmetic  204 us (31%)
  starting transfers between devices  196 us (30%)
  matrix products  123 us (19%)
  waiting for transfers between devices  94.6 us (14%)
  local copies, waits for them, and re-layouts  26.5 us (4%)
  between operations  8.42 us (1%)
    ppermute x124, starting transfers between devices, from_behind(): lax.ppermute(array, axis, [(i, (i + by) % devices) for i in range(devices)])  149 us
    scatter-add x15, other arithmetic, adjoint_step(): jax.ops.segment_sum(spread.reshape((-1,) + adjoint.shape[1:]), block_inde...  115 us
    add x60, other arithmetic, adjoint_step(): result + jax.ops.segment_sum(back, send_list[hop_id], num_segments=column...  75.4 us
    dot_general x16, matrix products, forward_step(): jnp.einsum('ckmj,ckij->cmi', picked, blocks, preferred_element_type=jnp.f...  69.3 us
    dot_general x15, matrix products, adjoint_step(): jnp.einsum('cmi,ckij->ckmj', rounded, blocks, preferred_element_type=jnp....  53.2 us
    ppermute x124, waiting for transfers between devices, from_behind(): lax.ppermute(array, axis, [(i, (i + by) % devices) for i in range(devices)])  48.3 us
    ppermute x14, starting transfers between devices, shifted(): return lax.ppermute(block, axis, route)  47.8 us
    ppermute x14, waiting for transfers between devices, shifted(): return lax.ppermute(block, axis, route)  46.3 us
  transfers between devices with their start and end apart: 138, of which 54 were waited for; matrix products, arithmetic and copies ran while one was open for 12% of the time, Pallas kernels for 0%

commit v1 on v0

v1 whole, which is shorter than its diff:
```python
import functools
import jax
import jax.numpy as jnp
from jax import lax
from jax.experimental import pallas as pl
from jax.experimental.pallas import tpu as pltpu
from jax.sharding import PartitionSpec as P

OFFSETS = (1, -1, 2, -2)
ROWS = 32
MESH = pl.DeviceIdType.MESH
F32 = jnp.float32
BF16 = jnp.bfloat16


class Tables:
    def __init__(self, cols, neigh, hops):
        blocks = cols * neigh
        self.source = 0
        self.perm = self.source + blocks
        self.column = self.perm + blocks
        self.keep = self.column + blocks
        self.last = self.keep + blocks
        self.reads = self.last + cols
        self.listed = self.reads + cols * hops
        self.send = self.listed + cols * hops


def index_tables(block_index, send_list):
    cols, neigh = block_index.shape
    hops = send_list.shape[0]
    blocks = cols * neigh
    flat = block_index.reshape(-1)
    number = jnp.arange(blocks, dtype=jnp.int32)
    key = flat * blocks + number
    rank = jnp.sum((key[None, :] < key[:, None]).astype(jnp.int32), axis=1)
    chosen = rank[None, :] == number[:, None]
    perm = jnp.sum(jnp.where(chosen, number[None, :], 0), axis=1)
    ordered = jnp.sum(jnp.where(chosen, flat[None, :], 0), axis=1)
    keep = jnp.concatenate([jnp.zeros((1,), jnp.int32), (ordered[1:] == ordered[:-1]).astype(jnp.int32)])
    column = jnp.arange(cols, dtype=jnp.int32)
    upto = jnp.sum((flat[None, :] <= column[:, None]).astype(jnp.int32), axis=1)
    own = jnp.sum((flat[None, :] == column[:, None]).astype(jnp.int32), axis=1)
    last = jnp.where(own > 0, upto - 1, blocks)
    source = jnp.where(flat < cols, flat, cols)
    hop = jnp.arange(hops, dtype=jnp.int32)
    reads = jnp.any(block_index[:, :, None] == (cols + hop)[None, None, :], axis=1).astype(jnp.int32)
    listed = (send_list[:, 0][None, :] == column[:, None]).astype(jnp.int32)
    parts = [source, perm, perm // neigh, keep, last, reads.reshape(-1), listed.reshape(-1), send_list.reshape(-1)]
    return jnp.concatenate(parts)


def kernel(
    sizes,
    tab, forcing, observed, jac_hbm, damping, error_weight, forcing_weight,
    traj, grad,
    jac, xin, xb, halo, halo_out, adj, adj_b, sums, back, back_out, cin, cout,
    jac_sem, halo_send, halo_recv, hand_send, hand_recv,
    back_send, back_recv, cin_send, cin_recv,
):
    space, count = sizes
    steps, cols, members, lev = forcing.shape
    neigh = jac[0].shape[0] // cols
    hops = halo.shape[1]
    blocks = cols * neigh
    at = Tables(cols, neigh, hops)
    me = lax.axis_index("space")
    turn = lax.axis_index("tm")
    is_first = turn == 0
    is_last = turn == count - 1
    group = max(g for g in range(1, min(cols, 6) + 1) if cols % g == 0)
    per = group * neigh

    def place(distance, later):
        return {"space": lax.rem(me + distance + 2 * space, space), "tm": turn + later}

    def jac_copy(s):
        return pltpu.make_async_copy(jac_hbm.at[s], jac[s], jac_sem.at[s])

    def halo_copy(s, hop, later, landing):
        return pltpu.make_async_remote_copy(
            src_ref=halo_out.at[s, hop], dst_ref=halo.at[landing, hop],
            send_sem=halo_send.at[s, hop], recv_sem=halo_recv.at[landing, hop],
            device_id=place(OFFSETS[hop], later), device_id_type=MESH)

    def hand_copy():
        return pltpu.make_async_remote_copy(
            src_ref=traj.at[steps - 1], dst_ref=xin, send_sem=hand_send, recv_sem=hand_recv,
            device_id=place(0, 1), device_id_type=MESH)

    def back_copy(s, hop, later, landing):
        return pltpu.make_async_remote_copy(
            src_ref=back_out.at[s, hop], dst_ref=back.at[landing, hop],
            send_sem=back_send.at[s, hop], recv_sem=back_recv.at[landing, hop],
            device_id=place(-OFFSETS[hop], later), device_id_type=MESH)

    def cin_copy():
        return pltpu.make_async_remote_copy(
            src_ref=cout, dst_ref=cin, send_sem=cin_send, recv_sem=cin_recv,
            device_id=place(0, -1), device_id_type=MESH)

    @pl.when(jnp.logical_not(is_first))
    def _():
        jac_copy(0).start()

    for s in range(1, steps):
        jac_copy(s).start()

    barrier = pltpu.get_barrier_semaphore()

    def greet(later):
        for distance in OFFSETS + ((0,) if later else ()):
            pl.semaphore_signal(barrier, inc=1, device_id=place(distance, later), device_id_type=MESH)

    greet(0)

    @pl.when(jnp.logical_not(is_first))
    def _():
        greet(-1)

    @pl.when(jnp.logical_not(is_last))
    def _():
        greet(1)

    for s in range(steps):
        xb[s, cols] = jnp.zeros((ROWS, lev), BF16)
    sums[blocks] = jnp.zeros((members, lev), F32)
    sides = jnp.where(is_first, 0, 1) + jnp.where(is_last, 0, 1)
    pl.semaphore_wait(barrier, hops + sides * (hops + 1))

    def scalar(index):
        return tab[index].astype(F32)

    def advance(s, before):
        def some(g, carry):
            for i in range(group):
                c = g * group + i
                picked = [xb[s, tab[at.source + c * neigh + k]] for k in range(neigh)]
                held = [jac[s][c * neigh + k] for k in range(neigh)]
                mixed = lax.dot_general(
                    jnp.concatenate(picked, axis=1), jnp.concatenate(held, axis=1),
                    (((1,), (1,)), ((), ())), preferred_element_type=F32)
                damp = damping[pl.ds(c, 1), :]
                traj[s, c] = damp * before[c] + forcing[s, c] + mixed[:members]
            return carry

        lax.fori_loop(0, cols // group, some, 0)
        remote = []
        for hop in range(hops):
            halo_copy(0, hop, 0, s).wait_recv()
        for hop in range(hops):
            block = tab[at.perm + blocks - hops + hop]
            remote.append(lax.dot_general(
                halo[s, hop], jac[s][block], (((1,), (1,)), ((), ())),
                preferred_element_type=F32)[:members])
        for c in range(cols):
            value = traj[s, c]
            for hop in range(hops):
                value = value + scalar(at.reads + c * hops + hop) * remote[hop]
            traj[s, c] = value

    def hand_on(s):
        for hop in range(hops):
            halo_out[s, hop, 0:members] = traj[s, tab[at.send + hop]].astype(BF16)
        if s < steps - 1:
            for hop in range(hops):
                halo_copy(s, hop, 0, s + 1).start()
            for c in range(cols):
                xb[s + 1, c, 0:members] = traj[s, c].astype(BF16)
        else:
            @pl.when(jnp.logical_not(is_last))
            def _():
                for hop in range(hops):
                    halo_copy(s, hop, 1, 0).start()
                hand_copy().start()

    @pl.when(is_first)
    def _():
        for c in range(cols):
            traj[0, c] = forcing[0, c]

    @pl.when(jnp.logical_not(is_first))
    def _():
        jac_copy(0).wait()
        hand_copy().wait_recv()
        for c in range(cols):
            xb[0, c, 0:members] = xin[c].astype(BF16)
        advance(0, xin)

    hand_on(0)
    for s in range(1, steps):
        jac_copy(s).wait()
        advance(s, traj.at[s - 1])
        hand_on(s)

    def misfit(s, c):
        return error_weight[pl.ds(c, 1), :] * (traj[s, c] - observed[s, c])

    def with_back(landing, c, value):
        for hop in range(hops):
            value = value + scalar(at.listed + c * hops + hop) * back[landing, hop]
        return value

    def keep_adjoint(s, c, value):
        adj[c] = value
        adj_b[c, 0:members] = value.astype(BF16)
        grad[s, c] = forcing_weight[...] * forcing[s, c] + value

    def transpose_step(s):
        for hop in range(hops):
            spot = blocks - hops + hop
            back_out[s, hop] = jnp.dot(
                adj_b[tab[at.column + spot]], jac[s][tab[at.perm + spot]],
                preferred_element_type=F32)[:members]
            if s > 0:
                back_copy(s, hop, 0, s - 1).start()
            else:
                back_copy(s, hop, -1, steps - 1).start()

        def some(g, total):
            for i in range(per):
                b = g * per + i
                spread = jnp.dot(
                    adj_b[tab[at.column + b]], jac[s][tab[at.perm + b]],
                    preferred_element_type=F32)[:members]
                total = spread + scalar(at.keep + b) * total
                sums[b] = total
            return total

        lax.fori_loop(0, cols // group, some, jnp.zeros((members, lev), F32))
        for c in range(cols):
            cout[c] = damping[pl.ds(c, 1), :] * adj[c] + sums[tab[at.last + c]]

    @pl.when(is_last)
    def _():
        for c in range(cols):
            keep_adjoint(steps - 1, c, misfit(steps - 1, c))

    @pl.when(jnp.logical_not(is_last))
    def _():
        for hop in range(hops):
            back_copy(0, hop, 0, steps - 1).wait_recv()
        cin_copy().wait_recv()
        for c in range(cols):
            keep_adjoint(steps - 1, c, with_back(steps - 1, c, misfit(steps - 1, c) + cin[c]))

    for s in range(steps - 1, 0, -1):
        transpose_step(s)
        for hop in range(hops):
            back_copy(0, hop, 0, s - 1).wait_recv()
        for c in range(cols):
            keep_adjoint(s - 1, c, with_back(s - 1, c, misfit(s - 1, c) + cout[c]))

    @pl.when(jnp.logical_not(is_first))
    def _():
        transpose_step(0)
        cin_copy().start()
        for hop in range(hops):
            back_copy(0, hop, -1, steps - 1).wait_send()
        cin_copy().wait_send()

    for s in range(1, steps):
        for hop in range(hops):
            back_copy(s, hop, 0, s - 1).wait_send()
            halo_copy(s - 1, hop, 0, s).wait_send()

    @pl.when(jnp.logical_not(is_last))
    def _():
        for hop in range(hops):
            halo_copy(steps - 1, hop, 1, 0).wait_send()
        hand_copy().wait_send()


def on_device(
    sizes, forcing, observed, jacobian, block_index, send_list, damping, error_weight, forcing_weight
):
    steps, cols, members, lev = forcing.shape
    neigh = jacobian.shape[2]
    hops = send_list.shape[0]
    blocks = cols * neigh
    tab = index_tables(block_index, send_list)
    vmem = pl.BlockSpec(memory_space=pltpu.VMEM)
    state = (cols, members, lev)
    dma = pltpu.SemaphoreType.DMA
    return pl.pallas_call(
        functools.partial(kernel, sizes),
        out_shape=(jax.ShapeDtypeStruct(forcing.shape, F32),) * 2,
        in_specs=[
            pl.BlockSpec(memory_space=pltpu.SMEM), vmem, vmem,
            pl.BlockSpec(memory_space=pl.ANY), vmem, vmem, vmem,
        ],
        out_specs=(vmem, vmem),
        scratch_shapes=[
            [pltpu.VMEM((blocks, lev, lev), BF16) for _ in range(steps)],
            pltpu.VMEM(state, F32),
            pltpu.VMEM((steps, cols + 1, ROWS, lev), BF16),
            pltpu.VMEM((steps, hops, ROWS, lev), BF16),
            pltpu.VMEM((steps, hops, ROWS, lev), BF16),
            pltpu.VMEM(state, F32),
            pltpu.VMEM((cols, ROWS, lev), BF16),
            pltpu.VMEM((blocks + 1, members, lev), F32),
            pltpu.VMEM((steps, hops, members, lev), F32),
            pltpu.VMEM((steps, hops, members, lev), F32),
            pltpu.VMEM(state, F32),
            pltpu.VMEM(state, F32),
            dma((steps,)),
            dma((steps, hops)), dma((steps, hops)), dma(()), dma(()),
            dma((steps, hops)), dma((steps, hops)), dma(()), dma(()),
        ],
        compiler_params=pltpu.CompilerParams(
            collective_id=0, has_side_effects=True, vmem_limit_bytes=48 * 1024 * 1024),
    )(
        tab, forcing, observed, jacobian.reshape(steps, blocks, lev, lev),
        damping, error_weight, forcing_weight.reshape(1, lev),
    )


def solution(mesh):
    sizes = (mesh.shape["space"], mesh.shape["tm"])
    in_specs = (
        P("tm", "space", None, None),
        P("tm", "space", None, None),
        P("tm", "space", None, None, None),
        P("space", None),
        P("space", None),
        P("space", None),
        P("space", None),
        P(),
    )
    out_specs = (P("tm", "space", None, None), P("tm", "space", None, None))
    return jax.shard_map(
        functools.partial(on_device, sizes), mesh=mesh, in_specs=in_specs, out_specs=out_specs,
        check_vma=False,
    )
```

time: 661 us -> 142 us (0.21)
  other arithmetic: 204 us -> 2.02 us
  starting transfers between devices: 196 us -> 0 us
  Pallas kernels: 0 us -> 131 us
  matrix products: 123 us -> 0 us
  waiting for transfers between devices: 94.6 us -> 0 us
  local copies, waits for them, and re-layouts: 26.5 us -> 7.96 us
  between operations: 8.42 us -> 0.7 us
    ppermute x138 -> x0, starting transfers between devices: 196 us -> none  [the longest x124 149 us: from_behind(): lax.ppermute(array, axis, [(i, (i + by) % devices) for i in range(devices)])]
    pallas_call x0 -> x1, Pallas kernels: none -> 131 us  [on_device(): pl.pallas_call(functools.partial(kernel, sizes), out_shape=(jax.ShapeDtyp...]
    dot_general x31 -> x0, matrix products: 123 us -> none  [the longest x16 69.3 us: forward_step(): jnp.einsum('ckmj,ckij->cmi', picked, blocks, preferred_element_type=jnp.f...]
    scatter-add x15 -> x0, other arithmetic: 115 us -> none  [adjoint_step(): jax.ops.segment_sum(spread.reshape((-1,) + adjoint.shape[1:]), block_inde...]
    ppermute x138 -> x0, waiting for transfers between devices: 94.6 us -> none  [the longest x124 48.3 us: from_behind(): lax.ppermute(array, axis, [(i, (i + by) % devices) for i in range(devices)])]
    add x76 -> x2, other arithmetic: 84 us -> 0.01 us  [the longest x1 0.01 us: index_tables(): key = flat * blocks + number]
    gather x32 -> x0, local copies, waits for them, and re-layouts: 13.9 us -> none  [the longest x16 13.6 us: forward_step(): picked = extended[block_index]]
  transfers between devices with their start and end apart: 138 -> 0, of which waited for: 54 -> 0; matrix products, arithmetic and copies ran while one was open for 12% -> 0% of each run, Pallas kernels for 0% -> 0%
where the time goes in v1:
time: 142 us; the launch traced here: 141 us
  Pallas kernels  131 us (92%)
  local copies, waits for them, and re-layouts  7.96 us (6%)
  other arithmetic  2.02 us (1%)
    pallas_call x1, Pallas kernels, on_device(): pl.pallas_call(functools.partial(kernel, sizes), out_shape=(jax.ShapeDtyp...  131 us
    unnamed x9, local copies, waits for them, and re-layouts  5.1 us

profile of v1, /device:TPU:0, one launch (start us, length us, event | category | flops | bytes accessed | tf_op | source)
XLA Modules:
  0.0 141.4 jit_solution(1877891995195662417)
XLA Ops:
  0.6 0.8 compare_reduce_fusion
  1.4 0.1 copy.22
  1.5 0.1 reshape.53
  1.6 0.7 fusion
  2.3 0.1 reshape.54
  2.4 0.8 copy.21
  3.1 0.1 reshape.50
  3.2 0.1 convert_reduce_fusion.1
  3.4 0.2 convert_reduce_fusion
  3.6 0.2 select_reduce_fusion
  3.7 0.1 compare_convert_fusion
  3.8 0.7 concatenate.3.tab
  4.6 1.1 copy.23.forcing
  5.7 1.1 copy.24.observed
  6.9 0.0 copy-start
  6.9 0.7 copy-done
  7.6 0.0 copy-start.1
  7.6 0.7 copy-done.1
  8.3 0.0 copy-start.2
  8.3 0.7 copy-done.2
  8.9 130.7 %shard_map.95 = (f32[2,24,20,128]{3,2,1,0:T(8,128)S(1)}, f32[2,24,20,128]{3,2,1,0:T(8,128)S(1)}) custom-call(s32[892]{0:T(1024)S(1)} %concatenate.3.tab, f32[2,24,20,128]{3,2,1,0:T(8,128)S(1)} %copy.23.forcing, f32[2,24,20,128]{3,2,1,0:T(8,128)S(1)} %copy.24.observed, bf16[2,168,128,128]{3,2,1,0:T(8,128)(2,1)} %bitcast.4, f32[24,128]{1,0:T(8,128)S(1)} %copy-done, ...), custom_call_target="tpu_custom_call" | custom-call | tf_op jit(solution)/shard_map/pallas_call | solution.py:285
  139.6 0.9 copy.25
  140.5 0.9 copy.26
  (5 shorter events, 0.0 us)
Async XLA Ops:
  6.9 0.7 copy-start
  7.6 0.7 copy-start.1
  8.3 0.7 copy-start.2

commit v2 on v1

--- a/solution.py
+++ b/solution.py
@@ -22,8 +22,8 @@
         self.keep = self.column + blocks
         self.last = self.keep + blocks
         self.reads = self.last + cols
-        self.listed = self.reads + cols * hops
-        self.send = self.listed + cols * hops
+        self.listed = self.reads + cols
+        self.send = self.listed + cols
 
 
 def index_tables(block_index, send_list):
@@ -44,9 +44,10 @@
     last = jnp.where(own > 0, upto - 1, blocks)
     source = jnp.where(flat < cols, flat, cols)
     hop = jnp.arange(hops, dtype=jnp.int32)
-    reads = jnp.any(block_index[:, :, None] == (cols + hop)[None, None, :], axis=1).astype(jnp.int32)
-    listed = (send_list[:, 0][None, :] == column[:, None]).astype(jnp.int32)
-    parts = [source, perm, perm // neigh, keep, last, reads.reshape(-1), listed.reshape(-1), send_list.reshape(-1)]
+    reads = jnp.any(block_index[:, :, None] == (cols + hop)[None, None, :], axis=1)
+    reads = jnp.sum(jnp.where(reads, 1 << hop, 0), axis=1)
+    listed = jnp.sum(jnp.where(send_list[:, 0][None, :] == column[:, None], 1 << hop, 0), axis=1)
+    parts = [source, perm, perm // neigh, keep, last, reads, listed, send_list.reshape(-1)]
     return jnp.concatenate(parts)
 
 
@@ -54,7 +55,7 @@
     sizes,
     tab, forcing, observed, jac_hbm, damping, error_weight, forcing_weight,
     traj, grad,
-    jac, xin, xb, halo, halo_out, adj, adj_b, sums, back, back_out, cin, cout,
+    misfit, subset, jac, xin, xb, halo, halo_out, adj, adj_b, sums, back, back_out, cin, cout,
     jac_sem, halo_send, halo_recv, hand_send, hand_recv,
     back_send, back_recv, cin_send, cin_recv,
 ):
@@ -68,8 +69,11 @@
     turn = lax.axis_index("tm")
     is_first = turn == 0
     is_last = turn == count - 1
-    group = max(g for g in range(1, min(cols, 6) + 1) if cols % g == 0)
-    per = group * neigh
+    pair = 2 if cols % 2 == 0 else 1
+    pairs = cols // pair
+    group = pairs // 2 if pairs % 2 == 0 else pairs
+    tiles = 4 if blocks % 4 == 0 else 1
+    half = blocks // tiles // 2 if blocks // tiles % 2 == 0 else blocks // tiles
 
     def place(distance, later):
         return {"space": lax.rem(me + distance + 2 * space, space), "tm": turn + later}
@@ -131,20 +135,33 @@
     def scalar(index):
         return tab[index].astype(F32)
 
+    def subset_sums(terms):
+        held = [jnp.zeros((members, lev), F32)]
+        for term in terms:
+            held = held + [term if i == 0 else value + term for i, value in enumerate(held)]
+        for i, value in enumerate(held):
+            subset[i] = value
+
     def advance(s, before):
         def some(g, carry):
             for i in range(group):
-                c = g * group + i
-                picked = [xb[s, tab[at.source + c * neigh + k]] for k in range(neigh)]
-                held = [jac[s][c * neigh + k] for k in range(neigh)]
+                first = (g * group + i) * pair
+                left, right = [], []
+                for c in range(pair):
+                    here = (first + c) * neigh
+                    left.append(jnp.concatenate([xb[s, tab[at.source + here + k]] for k in range(neigh)], axis=1))
+                    right.append(jnp.concatenate([jac[s][here + k] for k in range(neigh)], axis=1))
                 mixed = lax.dot_general(
-                    jnp.concatenate(picked, axis=1), jnp.concatenate(held, axis=1),
+                    jnp.concatenate(left, axis=0), jnp.concatenate(right, axis=0),
                     (((1,), (1,)), ((), ())), preferred_element_type=F32)
-                damp = damping[pl.ds(c, 1), :]
-                traj[s, c] = damp * before[c] + forcing[s, c] + mixed[:members]
+                for c in range(pair):
+                    column = first + c
+                    damp = damping[pl.ds(column, 1), :]
+                    own = mixed[c * ROWS : c * ROWS + members, c * lev : (c + 1) * lev]
+                    traj[s, column] = damp * before[column] + forcing[s, column] + own
             return carry
 
-        lax.fori_loop(0, cols // group, some, 0)
+        lax.fori_loop(0, pairs // group, some, 0)
         remote = []
         for hop in range(hops):
             halo_copy(0, hop, 0, s).wait_recv()
@@ -153,11 +170,12 @@
             remote.append(lax.dot_general(
                 halo[s, hop], jac[s][block], (((1,), (1,)), ((), ())),
                 preferred_element_type=F32)[:members])
-        for c in range(cols):
-            value = traj[s, c]
-            for hop in range(hops):
-                value = value + scalar(at.reads + c * hops + hop) * remote[hop]
+        subset_sums(remote)
+        for c in range(cols):
+            value = traj[s, c] + subset[tab[at.reads + c]]
             traj[s, c] = value
+            if s < steps - 1:
+                xb[s + 1, c, 0:members] = value.astype(BF16)
 
     def hand_on(s):
         for hop in range(hops):
@@ -165,8 +183,6 @@
         if s < steps - 1:
             for hop in range(hops):
                 halo_copy(s, hop, 0, s + 1).start()
-            for c in range(cols):
-                xb[s + 1, c, 0:members] = traj[s, c].astype(BF16)
         else:
             @pl.when(jnp.logical_not(is_last))
             def _():
@@ -178,6 +194,8 @@
     def _():
         for c in range(cols):
             traj[0, c] = forcing[0, c]
+            if steps > 1:
+                xb[1, c, 0:members] = forcing[0, c].astype(BF16)
 
     @pl.when(jnp.logical_not(is_first))
     def _():
@@ -193,13 +211,12 @@
         advance(s, traj.at[s - 1])
         hand_on(s)
 
-    def misfit(s, c):
-        return error_weight[pl.ds(c, 1), :] * (traj[s, c] - observed[s, c])
-
-    def with_back(landing, c, value):
-        for hop in range(hops):
-            value = value + scalar(at.listed + c * hops + hop) * back[landing, hop]
-        return value
+    for s in range(steps):
+        for c in range(cols):
+            misfit[s, c] = error_weight[pl.ds(c, 1), :] * (traj[s, c] - observed[s, c])
+
+    def add_back(landing):
+        subset_sums([back[landing, hop] for hop in range(hops)])
 
     def keep_adjoint(s, c, value):
         adj[c] = value
@@ -217,39 +234,56 @@
             else:
                 back_copy(s, hop, -1, steps - 1).start()
 
+        blank = jnp.zeros((ROWS, lev), BF16)
+
         def some(g, total):
-            for i in range(per):
-                b = g * per + i
-                spread = jnp.dot(
-                    adj_b[tab[at.column + b]], jac[s][tab[at.perm + b]],
-                    preferred_element_type=F32)[:members]
-                total = spread + scalar(at.keep + b) * total
-                sums[b] = total
+            for i in range(half):
+                first = (g * half + i) * tiles
+                turned = [adj_b[tab[at.column + first + n]] for n in range(tiles)]
+                held = [jac[s][tab[at.perm + first + n]] for n in range(tiles)]
+                if tiles == 4:
+                    left = [jnp.concatenate([w, blank], axis=1) for w in turned[:2]]
+                    left += [jnp.concatenate([blank, w], axis=1) for w in turned[2:]]
+                    left = jnp.concatenate(left, axis=0)
+                    upper = jnp.concatenate(held[:2], axis=1)
+                    lower = jnp.concatenate(held[2:], axis=1)
+                    right = jnp.concatenate([upper, lower], axis=0)
+                else:
+                    left, right = turned[0], held[0]
+                spread = jnp.dot(left, right, preferred_element_type=F32)
+                for n in range(tiles):
+                    lane = n % 2 * lev
+                    part = spread[n * ROWS : n * ROWS + members, lane : lane + lev]
+                    total = part + scalar(at.keep + first + n) * total
+                    sums[first + n] = total
             return total
 
-        lax.fori_loop(0, cols // group, some, jnp.zeros((members, lev), F32))
+        lax.fori_loop(0, blocks // tiles // half, some, jnp.zeros((members, lev), F32))
         for c in range(cols):
             cout[c] = damping[pl.ds(c, 1), :] * adj[c] + sums[tab[at.last + c]]
 
     @pl.when(is_last)
     def _():
         for c in range(cols):
-            keep_adjoint(steps - 1, c, misfit(steps - 1, c))
+            keep_adjoint(steps - 1, c, misfit[steps - 1, c])
 
     @pl.when(jnp.logical_not(is_last))
     def _():
         for hop in range(hops):
             back_copy(0, hop, 0, steps - 1).wait_recv()
+        add_back(steps - 1)
         cin_copy().wait_recv()
         for c in range(cols):
-            keep_adjoint(steps - 1, c, with_back(steps - 1, c, misfit(steps - 1, c) + cin[c]))
+            value = misfit[steps - 1, c] + cin[c] + subset[tab[at.listed + c]]
+            keep_adjoint(steps - 1, c, value)
 
     for s in range(steps - 1, 0, -1):
         transpose_step(s)
         for hop in range(hops):
             back_copy(0, hop, 0, s - 1).wait_recv()
-        for c in range(cols):
-            keep_adjoint(s - 1, c, with_back(s - 1, c, misfit(s - 1, c) + cout[c]))
+        add_back(s - 1)
+        for c in range(cols):
+            keep_adjoint(s - 1, c, misfit[s - 1, c] + cout[c] + subset[tab[at.listed + c]])
 
     @pl.when(jnp.logical_not(is_first))
     def _():
@@ -291,6 +325,8 @@
         ],
         out_specs=(vmem, vmem),
         scratch_shapes=[
+            pltpu.VMEM(forcing.shape, F32),
+            pltpu.VMEM((2 ** hops, members, lev), F32),
             [pltpu.VMEM((blocks, lev, lev), BF16) for _ in range(steps)],
             pltpu.VMEM(state, F32),
             pltpu.VMEM((steps, cols + 1, ROWS, lev), BF16),

time: 142 us -> 130 us (0.915)
  Pallas kernels: 131 us -> 119 us
    pallas_call x1, Pallas kernels: 131 us -> 119 us  [on_device(): pl.pallas_call(functools.partial(kernel, sizes), out_shape=(jax.ShapeDtyp...]
where the time goes in v2:
time: 130 us
  Pallas kernels  119 us (92%)
  local copies, waits for them, and re-layouts  7.68 us (6%)
  other arithmetic  2.1 us (2%)
    pallas_call x1, Pallas kernels, on_device(): pl.pallas_call(functools.partial(kernel, sizes), out_shape=(jax.ShapeDtyp...  119 us
    unnamed x9, local copies, waits for them, and re-layouts  5.1 us

profile of v2, /device:TPU:0, one launch (start us, length us, event | category | flops | bytes accessed | tf_op | source)
XLA Modules:
  0.0 129.8 jit_solution(16186315119666197016)
XLA Ops:
  0.6 0.8 compare_reduce_fusion
  1.4 0.7 select_reduce_fusion.2
  2.2 0.8 copy.21
  2.9 0.1 reshape.40
  3.0 0.1 convert_reduce_fusion.1
  3.2 0.2 convert_reduce_fusion
  3.4 0.2 select_reduce_fusion
  3.5 0.1 compare_convert_fusion
  3.6 0.7 concatenate.3.tab
  4.4 1.1 copy.22.forcing
  5.5 1.1 copy.23.observed
  6.6 0.0 copy-start
  6.7 0.7 copy-done
  7.4 0.0 copy-start.1
  7.4 0.7 copy-done.1
  8.1 0.0 copy-start.2
  8.1 0.7 copy-done.2
  8.7 119.3 %shard_map.95 = (f32[2,24,20,128]{3,2,1,0:T(8,128)S(1)}, f32[2,24,20,128]{3,2,1,0:T(8,128)S(1)}) custom-call(s32[748]{0:T(1024)S(1)} %concatenate.3.tab, f32[2,24,20,128]{3,2,1,0:T(8,128)S(1)} %copy.22.forcing, f32[2,24,20,128]{3,2,1,0:T(8,128)S(1)} %copy.23.observed, bf16[2,168,128,128]{3,2,1,0:T(8,128)(2,1)} %bitcast.4, f32[24,128]{1,0:T(8,128)S(1)} %copy-done, ...), custom_call_target="tpu_custom_call" | custom-call | tf_op jit(solution)/shard_map/pallas_call | solution.py:319
  128.0 0.9 copy.24
  128.9 0.9 copy.25
  (5 shorter events, 0.0 us)
Async XLA Ops:
  6.6 0.7 copy-start
  7.4 0.7 copy-start.1
  8.1 0.7 copy-start.2

commit v3 on v2

--- a/solution.py
+++ b/solution.py
@@ -53,14 +53,14 @@
 
 def kernel(
     sizes,
-    tab, forcing, observed, jac_hbm, damping, error_weight, forcing_weight,
-    traj, grad,
-    misfit, subset, jac, xin, xb, halo, halo_out, adj, adj_b, sums, back, back_out, cin, cout,
+    tab, forcing_hbm, observed_hbm, jac_hbm, damping_hbm, error_weight_hbm, forcing_weight_hbm,
+    traj_out, grad,
+    forcing, observed, damping, error_weight, forcing_weight, load_sem, traj, misfit, subset, jac, xin, xb, halo, halo_out, adj, adj_b, sums, back, back_out, cin, cout,
     jac_sem, halo_send, halo_recv, hand_send, hand_recv,
     back_send, back_recv, cin_send, cin_recv,
 ):
     space, count = sizes
-    steps, cols, members, lev = forcing.shape
+    steps, cols, members, lev = traj.shape
     neigh = jac[0].shape[0] // cols
     hops = halo.shape[1]
     blocks = cols * neigh
@@ -69,9 +69,7 @@
     turn = lax.axis_index("tm")
     is_first = turn == 0
     is_last = turn == count - 1
-    pair = 2 if cols % 2 == 0 else 1
-    pairs = cols // pair
-    group = pairs // 2 if pairs % 2 == 0 else pairs
+    group = cols // 2 if cols % 2 == 0 else cols
     tiles = 4 if blocks % 4 == 0 else 1
     half = blocks // tiles // 2 if blocks // tiles % 2 == 0 else blocks // tiles
 
@@ -109,6 +107,18 @@
 
     for s in range(1, steps):
         jac_copy(s).start()
+
+    loads = [
+        pltpu.make_async_copy(source, target, load_sem.at[i])
+        for i, (source, target) in enumerate([
+            (forcing_hbm, forcing), (damping_hbm, damping), (observed_hbm, observed),
+            (error_weight_hbm, error_weight), (forcing_weight_hbm, forcing_weight)])
+    ]
+    for load in loads:
+        load.start()
+
+    def rows(c):
+        return pl.ds(c, members, stride=cols)
 
     barrier = pltpu.get_barrier_semaphore()
 
@@ -145,23 +155,18 @@
     def advance(s, before):
         def some(g, carry):
             for i in range(group):
-                first = (g * group + i) * pair
-                left, right = [], []
-                for c in range(pair):
-                    here = (first + c) * neigh
-                    left.append(jnp.concatenate([xb[s, tab[at.source + here + k]] for k in range(neigh)], axis=1))
-                    right.append(jnp.concatenate([jac[s][here + k] for k in range(neigh)], axis=1))
-                mixed = lax.dot_general(
-                    jnp.concatenate(left, axis=0), jnp.concatenate(right, axis=0),
+                c = g * group + i
+                picked = [xb[s, tab[at.source + c * neigh + k]] for k in range(neigh)]
+                held = [jac[s][c * neigh + k] for k in range(neigh)]
+                turned = lax.dot_general(
+                    jnp.concatenate(held, axis=1), jnp.concatenate(picked, axis=1),
                     (((1,), (1,)), ((), ())), preferred_element_type=F32)
-                for c in range(pair):
-                    column = first + c
-                    damp = damping[pl.ds(column, 1), :]
-                    own = mixed[c * ROWS : c * ROWS + members, c * lev : (c + 1) * lev]
-                    traj[s, column] = damp * before[column] + forcing[s, column] + own
+                mixed = jnp.transpose(turned)[:members]
+                damp = damping[pl.ds(c, 1), :]
+                traj[s, c] = damp * before[c] + forcing[s, rows(c), :] + mixed
             return carry
 
-        lax.fori_loop(0, pairs // group, some, 0)
+        lax.fori_loop(0, cols // group, some, 0)
         remote = []
         for hop in range(hops):
             halo_copy(0, hop, 0, s).wait_recv()
@@ -190,12 +195,16 @@
                     halo_copy(s, hop, 1, 0).start()
                 hand_copy().start()
 
+    for load in loads:
+        load.wait()
+
     @pl.when(is_first)
     def _():
         for c in range(cols):
-            traj[0, c] = forcing[0, c]
+            value = forcing[0, rows(c), :]
+            traj[0, c] = value
             if steps > 1:
-                xb[1, c, 0:members] = forcing[0, c].astype(BF16)
+                xb[1, c, 0:members] = value.astype(BF16)
 
     @pl.when(jnp.logical_not(is_first))
     def _():
@@ -213,7 +222,8 @@
 
     for s in range(steps):
         for c in range(cols):
-            misfit[s, c] = error_weight[pl.ds(c, 1), :] * (traj[s, c] - observed[s, c])
+            misfit[s, c] = error_weight[pl.ds(c, 1), :] * (traj[s, c] - observed[s, rows(c), :])
+            traj_out[s, rows(c), :] = traj[s, c]
 
     def add_back(landing):
         subset_sums([back[landing, hop] for hop in range(hops)])
@@ -221,7 +231,7 @@
     def keep_adjoint(s, c, value):
         adj[c] = value
         adj_b[c, 0:members] = value.astype(BF16)
-        grad[s, c] = forcing_weight[...] * forcing[s, c] + value
+        grad[s, rows(c), :] = forcing_weight[...] * forcing[s, rows(c), :] + value
 
     def transpose_step(s):
         for hop in range(hops):
@@ -314,17 +324,27 @@
     blocks = cols * neigh
     tab = index_tables(block_index, send_list)
     vmem = pl.BlockSpec(memory_space=pltpu.VMEM)
+    far = pl.BlockSpec(memory_space=pl.ANY)
+    flat = (steps, members * cols, lev)
+
+    def by_member(array):
+        return array.transpose(0, 2, 1, 3).reshape(flat)
+
+    def by_column(array):
+        return array.reshape(steps, members, cols, lev).transpose(0, 2, 1, 3)
+
     state = (cols, members, lev)
     dma = pltpu.SemaphoreType.DMA
-    return pl.pallas_call(
+    trajectory, gradient = pl.pallas_call(
         functools.partial(kernel, sizes),
-        out_shape=(jax.ShapeDtypeStruct(forcing.shape, F32),) * 2,
-        in_specs=[
-            pl.BlockSpec(memory_space=pltpu.SMEM), vmem, vmem,
-            pl.BlockSpec(memory_space=pl.ANY), vmem, vmem, vmem,
-        ],
+        out_shape=(jax.ShapeDtypeStruct(flat, F32),) * 2,
+        in_specs=[pl.BlockSpec(memory_space=pltpu.SMEM)] + [far] * 6,
         out_specs=(vmem, vmem),
         scratch_shapes=[
+            pltpu.VMEM(flat, F32), pltpu.VMEM(flat, F32),
+            pltpu.VMEM((cols, lev), F32), pltpu.VMEM((cols, lev), F32), pltpu.VMEM((1, lev), F32),
+            dma((5,)),
+            pltpu.VMEM(forcing.shape, F32),
             pltpu.VMEM(forcing.shape, F32),
             pltpu.VMEM((2 ** hops, members, lev), F32),
             [pltpu.VMEM((blocks, lev, lev), BF16) for _ in range(steps)],
@@ -344,11 +364,12 @@
             dma((steps, hops)), dma((steps, hops)), dma(()), dma(()),
         ],
         compiler_params=pltpu.CompilerParams(
-            collective_id=0, has_side_effects=True, vmem_limit_bytes=48 * 1024 * 1024),
+            collective_id=0, has_side_effects=True, vmem_limit_bytes=63 * 1024 * 1024),
     )(
-        tab, forcing, observed, jacobian.reshape(steps, blocks, lev, lev),
+        tab, by_member(forcing), by_member(observed), jacobian.reshape(steps, blocks, lev, lev),
         damping, error_weight, forcing_weight.reshape(1, lev),
     )
+    return by_column(trajectory), by_column(gradient)
 
 
 def solution(mesh):

time: 130 us -> 131 us (level)
  Pallas kernels: 119 us -> 122 us
  local copies, waits for them, and re-layouts: 7.68 us -> 5.87 us
    pallas_call x1, Pallas kernels: 119 us -> 122 us  [on_device(): pl.pallas_call(functools.partial(kernel, sizes), out_shape=(jax.ShapeDtyp...]
    pallas_call x2 -> x0, local copies, waits for them, and re-layouts: 1.75 us -> none  [on_device(): pl.pallas_call(functools.partial(kernel, sizes), out_shape=(jax.ShapeDtyp...]
    unnamed x9 -> x3, local copies, waits for them, and re-layouts: 5.1 us -> 4.45 us
where the time goes in v3:
time: 131 us
  Pallas kernels  122 us (93%)
  local copies, waits for them, and re-layouts  5.87 us (4%)
  other arithmetic  2.1 us (2%)
    pallas_call x1, Pallas kernels, on_device(): pl.pallas_call(functools.partial(kernel, sizes), out_shape=(jax.ShapeDtyp...  122 us
    unnamed x3, local copies, waits for them, and re-layouts  4.45 us

profile of v3, /device:TPU:0, one launch (start us, length us, event | category | flops | bytes accessed | tf_op | source)
XLA Modules:
  0.0 130.7 jit_solution(6772413487420971534)
XLA Ops:
  0.6 0.8 compare_reduce_fusion
  1.4 0.7 select_reduce_fusion.2
  2.2 0.8 copy.13
  2.9 0.1 reshape.52
  3.0 0.1 convert_reduce_fusion.1
  3.2 0.2 convert_reduce_fusion
  3.4 0.2 select_reduce_fusion
  3.5 0.1 compare_convert_fusion
  3.6 1.3 %concatenate.3.tab = s32[748]{0:T(1024)} concatenate(s32[168]{0:T(256)S(1)} %get-tuple-element.13, s32[168]{0:T(256)S(1)} %get-tuple-element.9, s32[168]{0:T(256)S(1)} %and_select_fusion, s32[1]{0:T(128)} %constant.5.clone.1, s32[167]{0:T(256)S(1)} %compare_convert_fusion, s32[24]{0:T(128)S(1)} %compare_select_fusion.1, s32[24]{0:T(128)S(1)} %get-tuple-element.11, ...), dimensions={0} | concatenate | bytes 5984 | tf_op jit(solution)/shard_map/concatenate | solution.py:51
  5.0 122.0 %shard_map.95 = (f32[2,480,128]{2,1,0:T(8,128)}, f32[2,480,128]{2,1,0:T(8,128)}) custom-call(s32[748]{0:T(1024)} %concatenate.3.tab, f32[2,480,128]{2,1,0:T(8,128)} %bitcast.16, f32[2,480,128]{2,1,0:T(8,128)} %bitcast.17, bf16[2,168,128,128]{3,2,1,0:T(8,128)(2,1)} %bitcast.15, f32[24,128]{1,0:T(8,128)} %damping_hbm.1, f32[24,128]{1,0:T(8,128)} %error_weight_hbm.1, ...), custom_call_target="tpu_custom_call" | custom-call | tf_op jit(solution)/shard_map/pallas_call | solution.py:338
  127.0 1.8 %copy.16 = f32[2,24,20,128]{3,1,2,0:T(8,128)} copy(f32[2,24,20,128]{3,1,2,0:T(8,128)} %bitcast.19) | data formatting | bytes 983040
  128.8 1.8 %copy.17 = f32[2,24,20,128]{3,1,2,0:T(8,128)} copy(f32[2,24,20,128]{3,1,2,0:T(8,128)} %bitcast.18) | data formatting | bytes 983040
  (5 shorter events, 0.0 us)

commit v4 on v3

--- a/solution.py
+++ b/solution.py
@@ -176,15 +176,18 @@
                 halo[s, hop], jac[s][block], (((1,), (1,)), ((), ())),
                 preferred_element_type=F32)[:members])
         subset_sums(remote)
+        for hop in range(hops):
+            c = tab[at.send + hop]
+            value = traj[s, c] + subset[tab[at.reads + c]]
+            halo_out[s, hop, 0:members] = value.astype(BF16)
+        send_listed(s)
         for c in range(cols):
             value = traj[s, c] + subset[tab[at.reads + c]]
             traj[s, c] = value
             if s < steps - 1:
                 xb[s + 1, c, 0:members] = value.astype(BF16)
 
-    def hand_on(s):
-        for hop in range(hops):
-            halo_out[s, hop, 0:members] = traj[s, tab[at.send + hop]].astype(BF16)
+    def send_listed(s):
         if s < steps - 1:
             for hop in range(hops):
                 halo_copy(s, hop, 0, s + 1).start()
@@ -193,13 +196,21 @@
             def _():
                 for hop in range(hops):
                     halo_copy(s, hop, 1, 0).start()
+
+    def hand_on(s):
+        if s == steps - 1:
+            @pl.when(jnp.logical_not(is_last))
+            def _():
                 hand_copy().start()
 
-    for load in loads:
+    for load in loads[:2]:
         load.wait()
 
     @pl.when(is_first)
     def _():
+        for hop in range(hops):
+            halo_out[0, hop, 0:members] = forcing[0, rows(tab[at.send + hop]), :].astype(BF16)
+        send_listed(0)
         for c in range(cols):
             value = forcing[0, rows(c), :]
             traj[0, c] = value
@@ -220,6 +231,8 @@
         advance(s, traj.at[s - 1])
         hand_on(s)
 
+    for load in loads[2:]:
+        load.wait()
     for s in range(steps):
         for c in range(cols):
             misfit[s, c] = error_weight[pl.ds(c, 1), :] * (traj[s, c] - observed[s, rows(c), :])
@@ -228,22 +241,27 @@
     def add_back(landing):
         subset_sums([back[landing, hop] for hop in range(hops)])
 
-    def keep_adjoint(s, c, value):
-        adj[c] = value
-        adj_b[c, 0:members] = value.astype(BF16)
-        grad[s, rows(c), :] = forcing_weight[...] * forcing[s, rows(c), :] + value
-
-    def transpose_step(s):
+    def transpose_borders(s, value_of):
         for hop in range(hops):
             spot = blocks - hops + hop
+            value = value_of(tab[at.column + spot]).astype(BF16)
             back_out[s, hop] = jnp.dot(
-                adj_b[tab[at.column + spot]], jac[s][tab[at.perm + spot]],
-                preferred_element_type=F32)[:members]
+                value, jac[s][tab[at.perm + spot]], preferred_element_type=F32)
             if s > 0:
                 back_copy(s, hop, 0, s - 1).start()
             else:
                 back_copy(s, hop, -1, steps - 1).start()
 
+    def keep_adjoint(s, value_of):
+        for c in range(cols):
+            value = value_of(c)
+            adj[s, c] = value
+            adj_b[c, 0:members] = value.astype(BF16)
+
+    def own_part(s, c):
+        return damping[pl.ds(c, 1), :] * adj[s, c] + sums[tab[at.last + c]]
+
+    def transpose_step(s):
         blank = jnp.zeros((ROWS, lev), BF16)
 
         def some(g, total):
@@ -269,36 +287,63 @@
             return total
 
         lax.fori_loop(0, blocks // tiles // half, some, jnp.zeros((members, lev), F32))
-        for c in range(cols):
-            cout[c] = damping[pl.ds(c, 1), :] * adj[c] + sums[tab[at.last + c]]
+
+    top = steps - 1
 
     @pl.when(is_last)
     def _():
-        for c in range(cols):
-            keep_adjoint(steps - 1, c, misfit[steps - 1, c])
+        def value_of(c):
+            return misfit[top, c]
+
+        if top > 0:
+            transpose_borders(top, value_of)
+        keep_adjoint(top, value_of)
 
     @pl.when(jnp.logical_not(is_last))
     def _():
         for hop in range(hops):
-            back_copy(0, hop, 0, steps - 1).wait_recv()
-        add_back(steps - 1)
+            back_copy(0, hop, 0, top).wait_recv()
+        add_back(top)
         cin_copy().wait_recv()
-        for c in range(cols):
-            value = misfit[steps - 1, c] + cin[c] + subset[tab[at.listed + c]]
-            keep_adjoint(steps - 1, c, value)
-
-    for s in range(steps - 1, 0, -1):
+
+        def value_of(c):
+            return misfit[top, c] + cin[c] + subset[tab[at.listed + c]]
+
+        if top > 0:
+            transpose_borders(top, value_of)
+        keep_adjoint(top, value_of)
+
+    for s in range(top, 0, -1):
         transpose_step(s)
         for hop in range(hops):
             back_copy(0, hop, 0, s - 1).wait_recv()
         add_back(s - 1)
-        for c in range(cols):
-            keep_adjoint(s - 1, c, misfit[s - 1, c] + cout[c] + subset[tab[at.listed + c]])
+
+        def value_of(c, s=s):
+            return misfit[s - 1, c] + own_part(s, c) + subset[tab[at.listed + c]]
+
+        if s > 1:
+            transpose_borders(s - 1, value_of)
+        else:
+            @pl.when(jnp.logical_not(is_first))
+            def _():
+                transpose_borders(0, value_of)
+
+        keep_adjoint(s - 1, value_of)
 
     @pl.when(jnp.logical_not(is_first))
     def _():
         transpose_step(0)
+        for c in range(cols):
+            cout[c] = own_part(0, c)
         cin_copy().start()
+
+    for s in range(steps):
+        for c in range(cols):
+            grad[s, rows(c), :] = forcing_weight[...] * forcing[s, rows(c), :] + adj[s, c]
+
+    @pl.when(jnp.logical_not(is_first))
+    def _():
         for hop in range(hops):
             back_copy(0, hop, -1, steps - 1).wait_send()
         cin_copy().wait_send()
@@ -313,6 +358,15 @@
         for hop in range(hops):
             halo_copy(steps - 1, hop, 1, 0).wait_send()
         hand_copy().wait_send()
+
+
+def copy_kernel(first_in, second_in, first_out, second_out, sem):
+    first = pltpu.make_async_copy(first_in, first_out, sem.at[0])
+    second = pltpu.make_async_copy(second_in, second_out, sem.at[1])
+    first.start()
+    second.start()
+    first.wait()
+    second.wait()
 
 
 def on_device(
@@ -352,7 +406,7 @@
             pltpu.VMEM((steps, cols + 1, ROWS, lev), BF16),
             pltpu.VMEM((steps, hops, ROWS, lev), BF16),
             pltpu.VMEM((steps, hops, ROWS, lev), BF16),
-            pltpu.VMEM(state, F32),
+            pltpu.VMEM(forcing.shape, F32),
             pltpu.VMEM((cols, ROWS, lev), BF16),
             pltpu.VMEM((blocks + 1, members, lev), F32),
             pltpu.VMEM((steps, hops, members, lev), F32),
@@ -369,6 +423,14 @@
         tab, by_member(forcing), by_member(observed), jacobian.reshape(steps, blocks, lev, lev),
         damping, error_weight, forcing_weight.reshape(1, lev),
     )
+    trajectory, gradient = pl.pallas_call(
+        copy_kernel,
+        out_shape=(jax.ShapeDtypeStruct(flat, F32),) * 2,
+        in_specs=[far, far],
+        out_specs=(far, far),
+        scratch_shapes=[dma((2,))],
+        compiler_params=pltpu.CompilerParams(vmem_limit_bytes=63 * 1024 * 1024),
+    )(trajectory, gradient)
     return by_column(trajectory), by_column(gradient)
 
 

time: 131 us -> 156 us (1.19)
  Pallas kernels: 122 us -> 150 us
  local copies, waits for them, and re-layouts: 5.87 us -> 2.19 us
    pallas_call x0 -> x1, Pallas kernels: none -> 30.9 us  [on_device(): pl.pallas_call(copy_kernel, out_shape=(jax.ShapeDtypeStruct(flat, F32),)...]
    unnamed x3 -> x1, local copies, waits for them, and re-layouts: 4.45 us -> 0.76 us
    pallas_call x1, Pallas kernels: 122 us -> 119 us  [on_device(): pl.pallas_call(functools.partial(kernel, sizes), out_shape=(jax.ShapeDtyp...]
where the time goes in v4:
time: 156 us; the launch traced here: 155 us
  Pallas kernels  150 us (96%)
  local copies, waits for them, and re-layouts  2.19 us (1%)
  other arithmetic  2.1 us (1%)
    pallas_call x1, Pallas kernels, on_device(): pl.pallas_call(functools.partial(kernel, sizes), out_shape=(jax.ShapeDtyp...  119 us
    pallas_call x1, Pallas kernels, on_device(): pl.pallas_call(copy_kernel, out_shape=(jax.ShapeDtypeStruct(flat, F32),)...  30.9 us

profile of v4, /device:TPU:0, one launch (start us, length us, event | category | flops | bytes accessed | tf_op | source)
XLA Modules:
  0.0 155.3 jit_solution(6189292452465232587)
XLA Ops:
  0.6 0.8 compare_reduce_fusion
  1.4 0.7 select_reduce_fusion.2
  2.2 0.8 copy.13
  2.9 0.1 reshape.52
  3.0 0.1 convert_reduce_fusion.1
  3.2 0.2 convert_reduce_fusion
  3.4 0.2 select_reduce_fusion
  3.5 0.1 compare_convert_fusion
  3.6 1.3 concatenate.3.tab
  5.0 119.5 %shard_map.95 = (f32[2,480,128]{2,1,0:T(8,128)}, f32[2,480,128]{2,1,0:T(8,128)}) custom-call(s32[748]{0:T(1024)} %concatenate.3.tab, f32[2,480,128]{2,1,0:T(8,128)} %bitcast.16, f32[2,480,128]{2,1,0:T(8,128)} %bitcast.17, bf16[2,168,128,128]{3,2,1,0:T(8,128)(2,1)} %bitcast.15, f32[24,128]{1,0:T(8,128)} %damping_hbm.1, f32[24,128]{1,0:T(8,128)} %error_weight_hbm.1, ...), custom_call_target="tpu_custom_call" | custom-call | tf_op jit(solution)/shard_map/pallas_call | solution.py:392
  124.4 30.9 %shard_map.96 = (f32[2,480,128]{2,1,0:T(8,128)}, f32[2,480,128]{2,1,0:T(8,128)}) custom-call(f32[2,480,128]{2,1,0:T(8,128)} %get-tuple-element.6.first_in, f32[2,480,128]{2,1,0:T(8,128)} %get-tuple-element.7.second_in), custom_call_target="tpu_custom_call" | custom-call | tf_op jit(solution)/shard_map/pallas_call | solution.py:426
  (5 shorter events, 0.0 us)

commit v5 on v4

--- a/solution.py
+++ b/solution.py
@@ -69,7 +69,8 @@
     turn = lax.axis_index("tm")
     is_first = turn == 0
     is_last = turn == count - 1
-    group = cols // 2 if cols % 2 == 0 else cols
+    stack = 4 if cols % 4 == 0 else 1
+    group = cols // stack // 2 if cols // stack % 2 == 0 else cols // stack
     tiles = 4 if blocks % 4 == 0 else 1
     half = blocks // tiles // 2 if blocks // tiles % 2 == 0 else blocks // tiles
 
@@ -153,20 +154,31 @@
             subset[i] = value
 
     def advance(s, before):
+        lanes = lax.broadcasted_iota(jnp.int32, (lev, stack * ROWS), 1) // ROWS
+
         def some(g, carry):
             for i in range(group):
-                c = g * group + i
-                picked = [xb[s, tab[at.source + c * neigh + k]] for k in range(neigh)]
-                held = [jac[s][c * neigh + k] for k in range(neigh)]
+                first = (g * group + i) * stack
+                left, right = [], []
+                for r in range(stack):
+                    here = (first + r) * neigh
+                    left.append(jnp.concatenate([jac[s][here + k] for k in range(neigh)], axis=1))
+                    right.append(jnp.concatenate([xb[s, tab[at.source + here + k]] for k in range(neigh)], axis=1))
                 turned = lax.dot_general(
-                    jnp.concatenate(held, axis=1), jnp.concatenate(picked, axis=1),
+                    jnp.concatenate(left, axis=0), jnp.concatenate(right, axis=0),
                     (((1,), (1,)), ((), ())), preferred_element_type=F32)
-                mixed = jnp.transpose(turned)[:members]
-                damp = damping[pl.ds(c, 1), :]
-                traj[s, c] = damp * before[c] + forcing[s, rows(c), :] + mixed
+                chosen = turned[:lev]
+                for r in range(1, stack):
+                    chosen = jnp.where(lanes == r, turned[r * lev : (r + 1) * lev], chosen)
+                mixed = jnp.transpose(chosen)
+                for r in range(stack):
+                    c = first + r
+                    damp = damping[pl.ds(c, 1), :]
+                    own = mixed[r * ROWS : r * ROWS + members]
+                    traj[s, c] = damp * before[c] + forcing[s, rows(c), :] + own
             return carry
 
-        lax.fori_loop(0, cols // group, some, 0)
+        lax.fori_loop(0, cols // stack // group, some, 0)
         remote = []
         for hop in range(hops):
             halo_copy(0, hop, 0, s).wait_recv()
@@ -360,13 +372,22 @@
         hand_copy().wait_send()
 
 
-def copy_kernel(first_in, second_in, first_out, second_out, sem):
-    first = pltpu.make_async_copy(first_in, first_out, sem.at[0])
-    second = pltpu.make_async_copy(second_in, second_out, sem.at[1])
-    first.start()
-    second.start()
-    first.wait()
-    second.wait()
+def copy_kernel(first_in, second_in, first_out, second_out, first, second, sem):
+    loads = [
+        pltpu.make_async_copy(first_in, first, sem.at[0]),
+        pltpu.make_async_copy(second_in, second, sem.at[1]),
+    ]
+    stores = [
+        pltpu.make_async_copy(first, first_out, sem.at[2]),
+        pltpu.make_async_copy(second, second_out, sem.at[3]),
+    ]
+    for load in loads:
+        load.start()
+    for load, store in zip(loads, stores):
+        load.wait()
+        store.start()
+    for store in stores:
+        store.wait()
 
 
 def on_device(
@@ -428,7 +449,7 @@
         out_shape=(jax.ShapeDtypeStruct(flat, F32),) * 2,
         in_specs=[far, far],
         out_specs=(far, far),
-        scratch_shapes=[dma((2,))],
+        scratch_shapes=[pltpu.VMEM(flat, F32), pltpu.VMEM(flat, F32), dma((4,))],
         compiler_params=pltpu.CompilerParams(vmem_limit_bytes=63 * 1024 * 1024),
     )(trajectory, gradient)
     return by_column(trajectory), by_column(gradient)

time: 156 us -> 128 us (0.82)
  Pallas kernels: 150 us -> 122 us
    pallas_call x1, Pallas kernels: 30.9 us -> 2 us  [on_device(): pl.pallas_call(copy_kernel, out_shape=(jax.ShapeDtypeStruct(flat, F32),)...]
where the time goes in v5:
time: 128 us; the launch traced here: 127 us
  Pallas kernels  122 us (95%)
  local copies, waits for them, and re-layouts  2.19 us (2%)
  other arithmetic  2.1 us (2%)
    pallas_call x1, Pallas kernels, on_device(): pl.pallas_call(functools.partial(kernel, sizes), out_shape=(jax.ShapeDtyp...  120 us

profile of v5, /device:TPU:0, one launch (start us, length us, event | category | flops | bytes accessed | tf_op | source)
XLA Modules:
  0.0 127.2 jit_solution(16902776173899460931)
XLA Ops:
  0.6 0.8 compare_reduce_fusion
  1.4 0.7 select_reduce_fusion.2
  2.2 0.8 copy.13
  2.9 0.1 reshape.52
  3.0 0.1 convert_reduce_fusion.1
  3.2 0.2 convert_reduce_fusion
  3.4 0.2 select_reduce_fusion
  3.5 0.1 compare_convert_fusion
  3.6 1.3 %concatenate.3.tab = s32[748]{0:T(1024)} concatenate(s32[168]{0:T(256)S(1)} %get-tuple-element.17, s32[168]{0:T(256)S(1)} %get-tuple-element.13, s32[168]{0:T(256)S(1)} %and_select_fusion, s32[1]{0:T(128)} %constant.5.clone.1, s32[167]{0:T(256)S(1)} %compare_convert_fusion, s32[24]{0:T(128)S(1)} %compare_select_fusion.1, s32[24]{0:T(128)S(1)} %get-tuple-element.15, ...), dimensions={0} | concatenate | bytes 5984 | tf_op jit(solution)/shard_map/concatenate | solution.py:51
  5.0 120.3 %shard_map.95 = (f32[2,480,128]{2,1,0:T(8,128)}, f32[2,480,128]{2,1,0:T(8,128)}) custom-call(s32[748]{0:T(1024)} %concatenate.3.tab, f32[2,480,128]{2,1,0:T(8,128)} %bitcast.16, f32[2,480,128]{2,1,0:T(8,128)} %bitcast.17, bf16[2,168,128,128]{3,2,1,0:T(8,128)(2,1)} %bitcast.15, f32[24,128]{1,0:T(8,128)} %damping_hbm.1, f32[24,128]{1,0:T(8,128)} %error_weight_hbm.1, ...), custom_call_target="tpu_custom_call" | custom-call | tf_op jit(solution)/shard_map/pallas_call | solution.py:413
  125.2 2.0 %shard_map.96 = (f32[2,480,128]{2,1,0:T(8,128)}, f32[2,480,128]{2,1,0:T(8,128)}) custom-call(f32[2,480,128]{2,1,0:T(8,128)} %get-tuple-element.6.first_in, f32[2,480,128]{2,1,0:T(8,128)} %get-tuple-element.7.second_in), custom_call_target="tpu_custom_call" | custom-call | tf_op jit(solution)/shard_map/pallas_call | solution.py:447
  (5 shorter events, 0.0 us)

commit v6 on v5

--- a/solution.py
+++ b/solution.py
@@ -55,7 +55,7 @@
     sizes,
     tab, forcing_hbm, observed_hbm, jac_hbm, damping_hbm, error_weight_hbm, forcing_weight_hbm,
     traj_out, grad,
-    forcing, observed, damping, error_weight, forcing_weight, load_sem, traj, misfit, subset, jac, xin, xb, halo, halo_out, adj, adj_b, sums, back, back_out, cin, cout,
+    forcing, observed, damping, error_weight, forcing_weight, load_sem, traj, misfit, subset, part, fix_out, fix_in, fix_send, fix_recv, jac, xin, xb, halo, halo_out, adj, adj_b, sums, back, back_out, cin, cout,
     jac_sem, halo_send, halo_recv, hand_send, hand_recv,
     back_send, back_recv, cin_send, cin_recv,
 ):
@@ -88,7 +88,12 @@
 
     def hand_copy():
         return pltpu.make_async_remote_copy(
-            src_ref=traj.at[steps - 1], dst_ref=xin, send_sem=hand_send, recv_sem=hand_recv,
+            src_ref=part, dst_ref=xin, send_sem=hand_send, recv_sem=hand_recv,
+            device_id=place(0, 1), device_id_type=MESH)
+
+    def fix_copy():
+        return pltpu.make_async_remote_copy(
+            src_ref=fix_out, dst_ref=fix_in, send_sem=fix_send, recv_sem=fix_recv,
             device_id=place(0, 1), device_id_type=MESH)
 
     def back_copy(s, hop, later, landing):
@@ -175,10 +180,11 @@
                     c = first + r
                     damp = damping[pl.ds(c, 1), :]
                     own = mixed[r * ROWS : r * ROWS + members]
-                    traj[s, c] = damp * before[c] + forcing[s, rows(c), :] + own
+                    part[c] = damp * before[c] + forcing[s, rows(c), :] + own
             return carry
 
         lax.fori_loop(0, cols // stack // group, some, 0)
+        hand_on(s)
         remote = []
         for hop in range(hops):
             halo_copy(0, hop, 0, s).wait_recv()
@@ -187,14 +193,22 @@
             remote.append(lax.dot_general(
                 halo[s, hop], jac[s][block], (((1,), (1,)), ((), ())),
                 preferred_element_type=F32)[:members])
+        if s == steps - 1:
+            for hop in range(hops):
+                fix_out[hop] = remote[hop]
+
+            @pl.when(jnp.logical_not(is_last))
+            def _():
+                fix_copy().start()
+
         subset_sums(remote)
         for hop in range(hops):
             c = tab[at.send + hop]
-            value = traj[s, c] + subset[tab[at.reads + c]]
+            value = part[c] + subset[tab[at.reads + c]]
             halo_out[s, hop, 0:members] = value.astype(BF16)
         send_listed(s)
         for c in range(cols):
-            value = traj[s, c] + subset[tab[at.reads + c]]
+            value = part[c] + subset[tab[at.reads + c]]
             traj[s, c] = value
             if s < steps - 1:
                 xb[s + 1, c, 0:members] = value.astype(BF16)
@@ -233,15 +247,17 @@
     def _():
         jac_copy(0).wait()
         hand_copy().wait_recv()
-        for c in range(cols):
-            xb[0, c, 0:members] = xin[c].astype(BF16)
+        fix_copy().wait_recv()
+        subset_sums([fix_in[hop] for hop in range(hops)])
+        for c in range(cols):
+            value = xin[c] + subset[tab[at.reads + c]]
+            xin[c] = value
+            xb[0, c, 0:members] = value.astype(BF16)
         advance(0, xin)
 
-    hand_on(0)
     for s in range(1, steps):
         jac_copy(s).wait()
         advance(s, traj.at[s - 1])
-        hand_on(s)
 
     for load in loads[2:]:
         load.wait()
@@ -370,6 +386,7 @@
         for hop in range(hops):
             halo_copy(steps - 1, hop, 1, 0).wait_send()
         hand_copy().wait_send()
+        fix_copy().wait_send()
 
 
 def copy_kernel(first_in, second_in, first_out, second_out, first, second, sem):
@@ -422,6 +439,9 @@
             pltpu.VMEM(forcing.shape, F32),
             pltpu.VMEM(forcing.shape, F32),
             pltpu.VMEM((2 ** hops, members, lev), F32),
+            pltpu.VMEM(state, F32),
+            pltpu.VMEM((hops, members, lev), F32), pltpu.VMEM((hops, members, lev), F32),
+            dma(()), dma(()),
             [pltpu.VMEM((blocks, lev, lev), BF16) for _ in range(steps)],
             pltpu.VMEM(state, F32),
             pltpu.VMEM((steps, cols + 1, ROWS, lev), BF16),

time: 128 us -> 125 us (0.977)
  Pallas kernels: 122 us -> 120 us
    pallas_call x1, Pallas kernels: 120 us -> 118 us  [on_device(): pl.pallas_call(functools.partial(kernel, sizes), out_shape=(jax.ShapeDtyp...]
where the time goes in v6:
time: 125 us
  Pallas kernels  120 us (96%)
  local copies, waits for them, and re-layouts  2.19 us (2%)
  other arithmetic  2.1 us (2%)
    pallas_call x1, Pallas kernels, on_device(): pl.pallas_call(functools.partial(kernel, sizes), out_shape=(jax.ShapeDtyp...  118 us

profile of v6, /device:TPU:0, one launch (start us, length us, event | category | flops | bytes accessed | tf_op | source)
XLA Modules:
  0.0 125.1 jit_solution(9816025675394951329)
XLA Ops:
  0.6 0.8 compare_reduce_fusion
  1.4 0.7 select_reduce_fusion.2
  2.2 0.8 copy.13
  2.9 0.1 reshape.52
  3.0 0.1 convert_reduce_fusion.1
  3.2 0.2 convert_reduce_fusion
  3.4 0.2 select_reduce_fusion
  3.5 0.1 compare_convert_fusion
  3.6 1.3 %concatenate.3.tab = s32[748]{0:T(1024)} concatenate(s32[168]{0:T(256)S(1)} %get-tuple-element.17, s32[168]{0:T(256)S(1)} %get-tuple-element.13, s32[168]{0:T(256)S(1)} %and_select_fusion, s32[1]{0:T(128)} %constant.5.clone.1, s32[167]{0:T(256)S(1)} %compare_convert_fusion, s32[24]{0:T(128)S(1)} %compare_select_fusion.1, s32[24]{0:T(128)S(1)} %get-tuple-element.15, ...), dimensions={0} | concatenate | bytes 5984 | tf_op jit(solution)/shard_map/concatenate | solution.py:51
  5.0 118.1 %shard_map.95 = (f32[2,480,128]{2,1,0:T(8,128)}, f32[2,480,128]{2,1,0:T(8,128)}) custom-call(s32[748]{0:T(1024)} %concatenate.3.tab, f32[2,480,128]{2,1,0:T(8,128)} %bitcast.16, f32[2,480,128]{2,1,0:T(8,128)} %bitcast.17, bf16[2,168,128,128]{3,2,1,0:T(8,128)(2,1)} %bitcast.15, f32[24,128]{1,0:T(8,128)} %damping_hbm.1, f32[24,128]{1,0:T(8,128)} %error_weight_hbm.1, ...), custom_call_target="tpu_custom_call" | custom-call | tf_op jit(solution)/shard_map/pallas_call | solution.py:430
  123.1 2.0 %shard_map.96 = (f32[2,480,128]{2,1,0:T(8,128)}, f32[2,480,128]{2,1,0:T(8,128)}) custom-call(f32[2,480,128]{2,1,0:T(8,128)} %get-tuple-element.6.first_in, f32[2,480,128]{2,1,0:T(8,128)} %get-tuple-element.7.second_in), custom_call_target="tpu_custom_call" | custom-call | tf_op jit(solution)/shard_map/pallas_call | solution.py:467
  (5 shorter events, 0.0 us)

commit v7 on v6

--- a/solution.py
+++ b/solution.py
@@ -69,8 +69,8 @@
     turn = lax.axis_index("tm")
     is_first = turn == 0
     is_last = turn == count - 1
-    stack = 4 if cols % 4 == 0 else 1
-    group = cols // stack // 2 if cols // stack % 2 == 0 else cols // stack
+    pair = 2 if cols % 2 == 0 else 1
+    group = cols // pair // 2 if cols // pair % 2 == 0 else cols // pair
     tiles = 4 if blocks % 4 == 0 else 1
     half = blocks // tiles // 2 if blocks // tiles % 2 == 0 else blocks // tiles
 
@@ -159,31 +159,25 @@
             subset[i] = value
 
     def advance(s, before):
-        lanes = lax.broadcasted_iota(jnp.int32, (lev, stack * ROWS), 1) // ROWS
-
         def some(g, carry):
             for i in range(group):
-                first = (g * group + i) * stack
+                first = (g * group + i) * pair
                 left, right = [], []
-                for r in range(stack):
+                for r in range(pair):
                     here = (first + r) * neigh
-                    left.append(jnp.concatenate([jac[s][here + k] for k in range(neigh)], axis=1))
-                    right.append(jnp.concatenate([xb[s, tab[at.source + here + k]] for k in range(neigh)], axis=1))
-                turned = lax.dot_general(
+                    left.append(jnp.concatenate([xb[s, tab[at.source + here + k]] for k in range(neigh)], axis=1))
+                    right.append(jnp.concatenate([jac[s][here + k] for k in range(neigh)], axis=1))
+                mixed = lax.dot_general(
                     jnp.concatenate(left, axis=0), jnp.concatenate(right, axis=0),
                     (((1,), (1,)), ((), ())), preferred_element_type=F32)
-                chosen = turned[:lev]
-                for r in range(1, stack):
-                    chosen = jnp.where(lanes == r, turned[r * lev : (r + 1) * lev], chosen)
-                mixed = jnp.transpose(chosen)
-                for r in range(stack):
+                for r in range(pair):
                     c = first + r
                     damp = damping[pl.ds(c, 1), :]
-                    own = mixed[r * ROWS : r * ROWS + members]
+                    own = mixed[r * ROWS : r * ROWS + members, r * lev : (r + 1) * lev]
                     part[c] = damp * before[c] + forcing[s, rows(c), :] + own
             return carry
 
-        lax.fori_loop(0, cols // stack // group, some, 0)
+        lax.fori_loop(0, cols // pair // group, some, 0)
         hand_on(s)
         remote = []
         for hop in range(hops):

time: 125 us -> 125 us (level)
  no operation moved by 1% of the time
where the time goes in v7:
time: 125 us; the launch traced here: 124 us
  Pallas kernels  119 us (95%)
  local copies, waits for them, and re-layouts  2.19 us (2%)
  other arithmetic  2.1 us (2%)
    pallas_call x1, Pallas kernels, on_device(): pl.pallas_call(functools.partial(kernel, sizes), out_shape=(jax.ShapeDtyp...  117 us

profile of v7, /device:TPU:0, one launch (start us, length us, event | category | flops | bytes accessed | tf_op | source)
XLA Modules:
  0.0 124.4 jit_solution(7918428850598425822)
XLA Ops:
  0.6 0.8 compare_reduce_fusion
  1.4 0.7 select_reduce_fusion.2
  2.2 0.8 copy.13
  2.9 0.1 reshape.52
  3.0 0.1 convert_reduce_fusion.1
  3.2 0.2 convert_reduce_fusion
  3.4 0.2 select_reduce_fusion
  3.5 0.1 compare_convert_fusion
  3.6 1.3 %concatenate.3.tab = s32[748]{0:T(1024)} concatenate(s32[168]{0:T(256)S(1)} %get-tuple-element.17, s32[168]{0:T(256)S(1)} %get-tuple-element.13, s32[168]{0:T(256)S(1)} %and_select_fusion, s32[1]{0:T(128)} %constant.5.clone.1, s32[167]{0:T(256)S(1)} %compare_convert_fusion, s32[24]{0:T(128)S(1)} %compare_select_fusion.1, s32[24]{0:T(128)S(1)} %get-tuple-element.15, ...), dimensions={0} | concatenate | bytes 5984 | tf_op jit(solution)/shard_map/concatenate | solution.py:51
  5.0 117.5 %shard_map.95 = (f32[2,480,128]{2,1,0:T(8,128)}, f32[2,480,128]{2,1,0:T(8,128)}) custom-call(s32[748]{0:T(1024)} %concatenate.3.tab, f32[2,480,128]{2,1,0:T(8,128)} %bitcast.16, f32[2,480,128]{2,1,0:T(8,128)} %bitcast.17, bf16[2,168,128,128]{3,2,1,0:T(8,128)(2,1)} %bitcast.15, f32[24,128]{1,0:T(8,128)} %damping_hbm.1, f32[24,128]{1,0:T(8,128)} %error_weight_hbm.1, ...), custom_call_target="tpu_custom_call" | custom-call | tf_op jit(solution)/shard_map/pallas_call | solution.py:424
  122.4 2.0 %shard_map.96 = (f32[2,480,128]{2,1,0:T(8,128)}, f32[2,480,128]{2,1,0:T(8,128)}) custom-call(f32[2,480,128]{2,1,0:T(8,128)} %get-tuple-element.6.first_in, f32[2,480,128]{2,1,0:T(8,128)} %get-tuple-element.7.second_in), custom_call_target="tpu_custom_call" | custom-call | tf_op jit(solution)/shard_map/pallas_call | solution.py:461
  (5 shorter events, 0.0 us)
